TPU v7x, 256 devices: a whole 4x4x8 slice. The times are simulated.
256 devices in a mesh: dp: 16 (over x, y), space: 16 (over z, core).
Axes of the slice: x: 4, y: 4, z: 8, core: 2. Of those that a mesh axis runs over, the one named last changes fastest.
Arguments:
- volume: bfloat16 [16, 32, 32, 32, 128], P('dp', 'space'), may hold values from -6 to 6
- weight: bfloat16 [27, 128, 256], replicated, may hold values from -0.109375 to 0.109375
- cotangent: bfloat16 [16, 32, 32, 32, 256], P('dp', 'space'), may hold values from -6 to 6
Outputs:
- activation: bfloat16 [16, 32, 32, 32, 256], P('dp', 'space')
- input_grad: bfloat16 [16, 32, 32, 32, 128], P('dp', 'space')
- weight_grad: float32 [256, 3456], P(('dp', 'space'))
All inputs are finite; a program needn't handle non-finite values.
Results may differ from a plain program's by a relative error of at most 0.0075.
Values may be sent and summed in bfloat16 or wider, within the bound.
No kernel may reach another device: no remote copies, remote signals or barrier semaphores. Data moves between devices by JAX's collectives and lax.ppermute only.
A program may use at most 128 MiB of HBM per device.

v0:
```python
import jax
import jax.numpy as jnp
from jax import lax
from jax.sharding import PartitionSpec as P


def with_halo(array, sides, width):
    for axis, dim in sides:
        size, length = (lax.axis_size(axis), array.shape[dim])
        up = [(i, (i + 1) % size) for i in range(size - 1)]
        down = [(j, i) for i, j in up]
        last = lax.slice_in_dim(array, length - width, length, axis=dim)
        initial = lax.slice_in_dim(array, 0, width, axis=dim)
        before = lax.ppermute(last, axis, up)
        after = lax.ppermute(initial, axis, down)
        array = jnp.concatenate([before, array, after], axis=dim)
    return array


def passed_along(value, axis, steps):
    count = lax.axis_size(axis)
    initial, last = (max(0, -steps), min(count, count - steps))
    return lax.ppermute(value, axis, [(source, source + steps) for source in range(initial, last)])


def tap_offsets(k):
    return (k // 9, k // 3 % 3, k % 3)


def shards(volume, weight, cotangent):
    samples, planes, side = (volume.shape[0], volume.shape[1], volume.shape[2])
    chan_in = volume.shape[4]
    chan_out = cotangent.shape[4]
    rows = samples * planes * side * side
    extended = with_halo(volume, (("space", 1),), 1)
    source = jnp.pad(extended, ((0, 0), (0, 0), (1, 1), (1, 1), (0, 0)))

    def taken_rows(k):
        kd, kh, kw = tap_offsets(k)
        return source[:, kd : kd + planes, kh : kh + side, kw : kw + side, :].reshape(rows, chan_in)

    unfolded = jnp.concatenate([taken_rows(k) for k in range(27)], axis=1)
    pre = jnp.dot(
        unfolded, weight.reshape(27 * chan_in, chan_out), preferred_element_type=jnp.float32
    )
    activation = jnp.where(pre >= 0, pre, 0.3 * pre).astype(jnp.bfloat16)
    activation = activation.reshape(samples, planes, side, side, chan_out)
    contract_out = (((1,), (1,)), ((), ()))
    grads_pad = jnp.pad(cotangent, ((0, 0), (1, 1), (1, 1), (1, 1), (0, 0)))
    back = jnp.zeros((rows, chan_in), jnp.float32)
    for k in range(27):
        kd, kh, kw = tap_offsets(k)
        shifted = grads_pad[
            :, 2 - kd : 2 - kd + planes, 2 - kh : 2 - kh + side, 2 - kw : 2 - kw + side, :
        ].reshape(rows, chan_out)
        back = back + lax.dot_general(
            shifted, weight[k], contract_out, preferred_element_type=jnp.float32
        )
    rim_rows = samples * side * side
    lower_rim = jnp.zeros((rim_rows, chan_in), jnp.float32)
    upper_rim = jnp.zeros((rim_rows, chan_in), jnp.float32)
    for kh in range(3):
        for kw in range(3):
            first = grads_pad[:, 1:2, 2 - kh : 2 - kh + side, 2 - kw : 2 - kw + side, :].reshape(
                rim_rows, chan_out
            )
            lower_rim = lower_rim + lax.dot_general(
                first, weight[3 * kh + kw], contract_out, preferred_element_type=jnp.float32
            )
            last = grads_pad[
                :, planes : planes + 1, 2 - kh : 2 - kh + side, 2 - kw : 2 - kw + side, :
            ].reshape(rim_rows, chan_out)
            upper_rim = upper_rim + lax.dot_general(
                last, weight[18 + 3 * kh + kw], contract_out, preferred_element_type=jnp.float32
            )
    lower_rim = lower_rim.reshape(samples, side, side, chan_in)
    upper_rim = upper_rim.reshape(samples, side, side, chan_in)
    from_below = passed_along(upper_rim.astype(jnp.bfloat16), "space", 1).astype(upper_rim.dtype)
    from_above = passed_along(lower_rim.astype(jnp.bfloat16), "space", -1).astype(lower_rim.dtype)
    middle = back.reshape(samples, planes, side, side, chan_in)
    middle = middle.at[:, 0].add(from_below)
    middle = middle.at[:, planes - 1].add(from_above)
    input_grad = middle.astype(jnp.bfloat16)
    flat_grads = cotangent.reshape(rows, chan_out)
    contract_rows = (((0,), (0,)), ((), ()))
    share = lax.psum_scatter(
        lax.dot_general(flat_grads, unfolded, contract_rows, preferred_element_type=jnp.float32),
        ("dp", "space"),
        scatter_dimension=0,
        tiled=True,
    )
    count_all = lax.axis_size("dp") * samples * lax.axis_size("space") * planes * side * side
    weight_grad = share / jnp.sqrt(jnp.float32(count_all))
    return (activation, input_grad, weight_grad)


def solution(mesh):
    in_specs = (P("dp", "space", None, None, None), P(), P("dp", "space", None, None, None))
    out_specs = (
        P("dp", "space", None, None, None),
        P("dp", "space", None, None, None),
        P(("dp", "space"), None),
    )
    return jax.shard_map(shards, mesh=mesh, in_specs=in_specs, out_specs=out_specs, check_vma=False)
```

profile of v0, /device:TPU:6, one launch (start us, length us, event | category | flops | bytes accessed | tf_op | source)
XLA Modules:
  0.0 362.1 jit_solution(16973350323378579682)
XLA Ops:
  7.2 6.5 %pad_slice_fusion = (bf16[1,1,32,32,256]{4,3,2,1,0:T(8,128)(2,1)S(1)}, bf16[1,1,32,32,256]{4,3,2,1,0:T(8,128)(2,1)S(1)}, bf16[1,1,32,32,256]{4,3,2,1,0:T(8,128)(...) fusion(bf16[1,2,32,32,256]{4,3,2,1,0:T(8,128)(2,1)} %param.9), kind=kLoop, calls=%fused_computation | loop fusion | bytes 11534336 | tf_op jit(solution)/shard_map/slice | solution.py:64
  16.2 1.0 fusion.7
  17.2 2.4 collective-permute-start.2
  22.1 1.0 fusion.8
  23.1 1.3 collective-permute-start.3
  24.4 0.8 fusion.106
  25.2 4.8 %collective-permute-start = (bf16[1,1,32,32,128]{4,3,2,1,0:T(8,128)(2,1)}, bf16[1,1,32,32,128]{4,3,2,1,0:T(8,128)(2,1)}, u32[]{:S(2)}, u32[]{:S(2)}) collective-permute-start(bf16[1,1,32,32,128]{4,3,2,1,0:T(8,128)(2,1)} %get-tuple-element.103), channel_id=1, source_target_pairs={{0,1},{1,2},{2,3},{3,4},{4,5},{5,6},{6,7},{7,8},{8,9},{9,10},{10,1... | collective-permute-start | bytes 786440 | tf_op jit(solution)/shard_map/ppermute | solution.py:14
  30.0 1.5 collective-permute-start.1
  31.5 7.9 %pad_slice_fusion.16 = (bf16[1,2,32,32,256]{4,3,2,1,0:T(8,128)(2,1)}, bf16[1,2,32,32,256]{4,3,2,1,0:T(8,128)(2,1)}, bf16[1,2,32,32,256]{4,3,2,1,0:T(8,128)(2,1)}...) fusion(bf16[1,2,32,32,256]{4,3,2,1,0:T(8,128)(2,1)S(1)} %copy-done), kind=kLoop, calls=%fused_computation.16 | loop fusion | bytes 20971520 | tf_op jit(solution)/shard_map/slice | solution.py:53
  39.4 2.3 pad_slice_fusion.17
  42.2 0.8 copy-done.9
  46.9 0.4 convolution_add_fusion.18
  47.3 0.4 convolution_add_fusion.17
  47.7 0.4 convolution_add_fusion.16
  49.0 0.4 convolution_add_fusion.13
  52.1 0.4 convolution_add_fusion.6
  53.0 0.4 convolution_add_fusion.4
  53.8 0.4 convolution_add_fusion.2
  54.3 1.4 convolution_add_fusion.1
  55.7 2.0 convolution_add_fusion
  57.7 1.6 select_maximum_fusion
  59.8 2.9 fusion.104
  63.2 1.1 pad_maximum_fusion
  67.4 5.0 %copy-done.10 = bf16[2048,3456]{1,0:T(8,128)(2,1)} copy-done((bf16[2048,3456]{1,0:T(8,128)(2,1)}, bf16[2048,3456]{1,0:T(8,128)(2,1)S(1)}, u32[]{:S(2)}) %copy-start.10) | copy-done | bytes 14155800
  72.5 6.0 %convolution_bitcast_fusion = f32[256,3456]{0,1:T(8,128)} fusion(bf16[2048,3456]{1,0:T(8,128)(2,1)S(1)} %constant_dynamic-update-slice_fusion, bf16[2048,256]{1,0:T(8,128)(2,1)S(1)} %bitcast.254), kind=kOutput, calls=%fused_computation.43 | convolution fusion | flops 3623878656 | bytes 18743296 | tf_op jit(solution)/shard_map/dot_general | solution.py:87
  78.5 1.2 fusion.10
  79.7 1.1 fusion.9
  80.8 0.9 convert_element_type.45
  81.7 10.1 %fusion.3 = bf16[2048,256]{1,0:T(8,128)(2,1)} fusion(bf16[2048,3456]{1,0:T(8,128)(2,1)} %copy-done.10, bf16[3456,256]{1,0:T(8,128)(2,1)S(1)} %bitcast.257), kind=kOutput, calls=%fused_computation.77 | convolution fusion | flops 3625975808 | bytes 16973824 | tf_op jit(solution)/shard_map/dot_general | solution.py:43
  91.8 260.3 %all-reduce.5.cloned.1.call-done = f32[256,3456]{0,1:T(8,128)} async-done(((f32[256,3456]{0,1:T(8,128)}), f32[256,3456]{0,1:T(8,128)}) %all-reduce.5.cloned.1.call-update) | async-done | bytes 3538960
  352.1 2.0 dynamic-slice_multiply_fusion
  354.1 1.1 copy.7
  (88 shorter events, 17.2 us)
Async XLA Ops:
  7.2 6.6 %copy-start.2 = (bf16[27,128,256]{2,1,0:T(8,128)(2,1)S(1)}, bf16[27,128,256]{2,1,0:T(8,128)(2,1)}, u32[]{:S(2)}) copy-start(bf16[27,128,256]{2,1,0:T(8,128)(2,1)} %param.8) | copy-start | bytes 5308420
  7.2 344.9 %all-reduce.5.cloned.1.call-start = ((), (), s32[]{:S(2)}) async-start(), calls=%async_computation | async-start | bytes 7077888
  17.2 61.2 %collective-permute-start.2 = (bf16[1,32,32,128]{3,2,1,0:T(8,128)(2,1)}, bf16[1,32,32,128]{3,2,1,0:T(8,128)(2,1)}, u32[]{:S(2)}, u32[]{:S(2)}) collective-permute-start(bf16[1,32,32,128]{3,2,1,0:T(8,128)(2,1)} %bitcast.93), channel_id=1, source_target_pairs={{0,1},{1,2},{2,3},{3,4},{4,5},{5,6},{6,7},{7,8},{8,9},{9,10},{10,1... | collective-permute-start | bytes 786440 | tf_op jit(solution)/shard_map/ppermute | solution.py:23
  21.2 3.2 copy-start.1
  21.5 10.0 %copy-start = (bf16[1,2,32,32,256]{4,3,2,1,0:T(8,128)(2,1)S(1)}, bf16[1,2,32,32,256]{4,3,2,1,0:T(8,128)(2,1)}, u32[]{:S(2)}) copy-start(bf16[1,2,32,32,256]{4,3,2,1,0:T(8,128)(2,1)} %param.9) | copy-start | bytes 3145732
  23.1 56.6 %collective-permute-start.3 = (bf16[1,32,32,128]{3,2,1,0:T(8,128)(2,1)}, bf16[1,32,32,128]{3,2,1,0:T(8,128)(2,1)}, u32[]{:S(2)}, u32[]{:S(2)}) collective-permute-start(bf16[1,32,32,128]{3,2,1,0:T(8,128)(2,1)} %bitcast.104), channel_id=1, source_target_pairs={{1,0},{2,1},{3,2},{4,3},{5,4},{6,5},{7,6},{8,7},{9,8},{10,9},{11,1... | collective-permute-start | bytes 786440 | tf_op jit(solution)/shard_map/ppermute | solution.py:23
  25.2 32.5 %collective-permute-start = (bf16[1,1,32,32,128]{4,3,2,1,0:T(8,128)(2,1)}, bf16[1,1,32,32,128]{4,3,2,1,0:T(8,128)(2,1)}, u32[]{:S(2)}, u32[]{:S(2)}) collective-permute-start(bf16[1,1,32,32,128]{4,3,2,1,0:T(8,128)(2,1)} %get-tuple-element.103), channel_id=1, source_target_pairs={{0,1},{1,2},{2,3},{3,4},{4,5},{5,6},{6,7},{7,8},{8,9},{9,10},{10,1... | collective-permute-start | bytes 786440 | tf_op jit(solution)/shard_map/ppermute | solution.py:14
  30.0 27.8 %collective-permute-start.1 = (bf16[1,1,32,32,128]{4,3,2,1,0:T(8,128)(2,1)}, bf16[1,1,32,32,128]{4,3,2,1,0:T(8,128)(2,1)}, u32[]{:S(2)}, u32[]{:S(2)}) collective-permute-start(bf16[1,1,32,32,128]{4,3,2,1,0:T(8,128)(2,1)} %get-tuple-element.104), channel_id=1, source_target_pairs={{1,0},{2,1},{3,2},{4,3},{5,4},{6,5},{7,6},{8,7},{9,8},{10,9},{11,1... | collective-permute-start | bytes 786440 | tf_op jit(solution)/shard_map/ppermute | solution.py:15
  41.7 1.2 copy-start.9
  41.7 1.7 copy-start.8
  42.9 1.3 copy-start.7
  43.4 1.3 copy-start.6
  44.2 1.3 copy-start.5
  44.7 1.3 copy-start.4
  67.4 5.0 %copy-start.10 = (bf16[2048,3456]{1,0:T(8,128)(2,1)}, bf16[2048,3456]{1,0:T(8,128)(2,1)S(1)}, u32[]{:S(2)}) copy-start(bf16[2048,3456]{1,0:T(8,128)(2,1)S(1)} %constant_dynamic-update-slice_fusion) | copy-start | bytes 42467332
  78.4 3.2 copy-start.3
Sparse Core Ops, SparseCore 0:
  78.6 273.4 all-reduce.4
where the time goes:
time: 363 us; the launch traced here: 362 us
  waiting for transfers between devices  260 us (72%)
  matrix products  37.1 us (10%)
  local copies, waits for them, and re-layouts  32.2 us (9%)
  between operations  14.6 us (4%)
  starting transfers between devices  9.96 us (3%)
  other arithmetic  7.91 us (2%)
    unnamed x2, waiting for transfers between devices  260 us
    dot_general x27, matrix products, shards(): lax.dot_general(shifted, weight[k], contract_out, preferred_element_type=...  14.2 us
    unnamed x49, local copies, waits for them, and re-layouts  11.1 us
    slice x2, local copies, waits for them, and re-layouts, shards(): grads_pad[:, 2 - kd:2 - kd + planes, 2 - kh:2 - kh + side, 2 - kw:2 - kw...  10.2 us
    dot_general x1, matrix products, shards(): jnp.dot(unfolded, weight.reshape(27 * chan_in, chan_out), preferred_eleme...  10.1 us
  transfers between devices with their start and end apart: 5, of which 1 were waited for; matrix products, arithmetic and copies ran while one was open for 16% of the time, Pallas kernels for 0%

commit v1 on v0

v1 whole, which is shorter than its diff:
```python
import jax
import jax.numpy as jnp
from jax import lax
from jax.experimental import pallas as pl
from jax.experimental.pallas import tpu as pltpu
from jax.sharding import PartitionSpec as P

bf16, f32 = jnp.bfloat16, jnp.float32
SIDE = 32
CELLS = SIDE * SIDE
CIN, COUT, TAPS = 128, 256, 27
SLAB = 2
PADDED = CELLS + 2 * SIDE
ROWS = 256
VMEM_LIMIT = 48 << 20
FLOPS = 2 * SLAB * CELLS * TAPS * CIN * COUT


def in_vmem():
    return pl.BlockSpec(memory_space=pltpu.VMEM)


def call(kernel, name, outs, scratch, args):
    single = not isinstance(outs, tuple)
    return pl.pallas_call(
        kernel,
        out_shape=outs,
        in_specs=[in_vmem()] * len(args),
        out_specs=in_vmem() if single else tuple(in_vmem() for _ in outs),
        scratch_shapes=scratch,
        compiler_params=pltpu.CompilerParams(vmem_limit_bytes=VMEM_LIMIT),
        cost_estimate=pl.CostEstimate(flops=FLOPS, bytes_accessed=5 << 20, transcendentals=0),
        name=name,
    )(*args)


def product(a, b):
    return jnp.dot(a, b, preferred_element_type=f32)


def fill_taps(planes, wide, taps):
    col = lax.broadcasted_iota(jnp.int32, (CELLS, CIN), 0) % SIDE
    zero = jnp.zeros((SIDE, 3 * CIN), bf16)
    inner = pl.ds(SIDE, CELLS)
    for i, plane in enumerate(planes):
        wide[pl.ds(8, CELLS), :] = plane[...].astype(f32)
        taps[i, pl.ds(0, SIDE), :] = zero
        taps[i, pl.ds(SIDE + CELLS, SIDE), :] = zero
        left = jnp.where(col > 0, wide[pl.ds(7, CELLS), :], 0.0)
        right = jnp.where(col < SIDE - 1, wide[pl.ds(9, CELLS), :], 0.0)
        taps[i, inner, pl.ds(0, CIN)] = left.astype(bf16)
        taps[i, inner, pl.ds(CIN, CIN)] = plane[...]
        taps[i, inner, pl.ds(2 * CIN, CIN)] = right.astype(bf16)


def taps_scratch():
    return [pltpu.VMEM((CELLS + 16, CIN), f32), pltpu.VMEM((SLAB + 2, PADDED, 3 * CIN), bf16)]


def weight_grad_kernel(order, before, volume, after, cot, keep, send, wide, taps, turned):
    fill_taps((before, volume.at[0], volume.at[1], after), wide, taps)
    for j in range(SLAB * CELLS // 256):
        rows = pl.ds(j * 256, 256)
        turned[:, rows] = lax.dot_general(
            order[...], cot[rows, :], (((1,), (1,)), ((), ())), preferred_element_type=f32
        ).astype(bf16)
    for first in range(0, TAPS, 2):
        some = range(first, min(first + 2, TAPS))
        total = None
        for d in range(SLAB):
            parts = [
                taps[d + k // 9, pl.ds(k // 3 % 3 * SIDE, CELLS), pl.ds(k % 3 * CIN, CIN)] for k in some
            ]
            part = product(turned[:, pl.ds(d * CELLS, CELLS)], jnp.concatenate(parts, axis=1))
            total = part if total is None else total + part
        lanes = pl.ds(first * CIN, len(some) * CIN)
        keep[:, lanes] = total[: COUT // 2]
        send[:, lanes] = total[COUT // 2 :].astype(bf16)


def weight_grad_share(order, before, volume, after, cot):
    half = (COUT // 2, TAPS * CIN)
    return call(
        weight_grad_kernel,
        "weight_grad",
        (jax.ShapeDtypeStruct(half, f32), jax.ShapeDtypeStruct(half, bf16)),
        taps_scratch() + [pltpu.VMEM((COUT, SLAB * CELLS), bf16)],
        (order, before, volume, after, cot),
    )


def forward_kernel(before, volume, after, weight, out, wide, taps):
    fill_taps((before, volume.at[0], volume.at[1], after), wide, taps)
    for d in range(SLAB):

        def step(i, carry):
            base = pl.multiple_of(i * ROWS, ROWS)
            parts = [
                taps[
                    d + k // 9,
                    pl.ds(pl.multiple_of(base + k // 3 % 3 * SIDE, SIDE), ROWS),
                    pl.ds(k % 3 * CIN, CIN),
                ]
                for k in range(TAPS)
            ]
            pre = product(jnp.concatenate(parts, axis=1), weight[...])
            out[pl.ds(d * CELLS + base, ROWS), :] = jnp.where(pre >= 0, pre, 0.3 * pre).astype(bf16)
            return carry

        lax.fori_loop(0, CELLS // ROWS, step, 0)


def forward(before, volume, after, weight):
    return call(
        forward_kernel,
        "forward",
        jax.ShapeDtypeStruct((SLAB * CELLS, COUT), bf16),
        taps_scratch(),
        (before, volume, after, weight),
    )


def input_grad_kernel(before, cot, after, weight, out, padded, turned, sums):
    zero = jnp.zeros((SIDE, COUT), bf16)
    for i, plane in enumerate((before, cot.at[pl.ds(0, CELLS)], cot.at[pl.ds(CELLS, CELLS)], after)):
        padded[i, pl.ds(0, SIDE), :] = zero
        padded[i, pl.ds(SIDE + CELLS, SIDE), :] = zero
        padded[i, pl.ds(SIDE, CELLS), :] = plane[...]
    for k in range(TAPS):
        turned[pl.ds(k // 3 * COUT, COUT), pl.ds(k % 3 * CIN, CIN)] = weight[pl.ds(k * CIN, CIN), :].T
    col = lax.broadcasted_iota(jnp.int32, (ROWS, CIN), 0) % SIDE
    for d in range(SLAB):

        def step(i, carry):
            base = pl.multiple_of(i * ROWS, ROWS)
            parts = [
                padded[d + 2 - j // 3, pl.ds(pl.multiple_of(base + (2 - j % 3) * SIDE, SIDE), ROWS), :]
                for j in range(9)
            ]
            sums[pl.ds(8, ROWS), :] = product(jnp.concatenate(parts, axis=1), turned[...])
            total = sums[pl.ds(8, ROWS), pl.ds(CIN, CIN)]
            total = total + jnp.where(col < SIDE - 1, sums[pl.ds(9, ROWS), pl.ds(0, CIN)], 0.0)
            total = total + jnp.where(col > 0, sums[pl.ds(7, ROWS), pl.ds(2 * CIN, CIN)], 0.0)
            out[pl.ds(d * CELLS + base, ROWS), :] = total.astype(bf16)
            return carry

        lax.fori_loop(0, CELLS // ROWS, step, 0)


def input_grad_of(before, cot, after, weight):
    return call(
        input_grad_kernel,
        "input_grad",
        jax.ShapeDtypeStruct((SLAB * CELLS, CIN), bf16),
        [
            pltpu.VMEM((SLAB + 2, PADDED, COUT), bf16),
            pltpu.VMEM((9 * COUT, 3 * CIN), bf16),
            pltpu.VMEM((ROWS + 16, 3 * CIN), f32),
        ],
        (before, cot, after, weight),
    )


def neighbours(value, step):
    pairs = [(i, i + step) for i in range(16) if 0 <= i + step < 16]
    return lax.ppermute(value, "space", pairs)


def moved(x, y, z, c, bits):
    b = bits
    c = c ^ b[0]
    first, second = b[1] ^ (3 * b[3]), b[2] ^ (3 * b[4])
    x = x ^ (first + (second - first) * c)
    y = y ^ (second + (first - second) * c)
    return x, y, z ^ (b[5] + 2 * b[6] + 4 * b[7]), c


def partners(stage):
    bits = [int(i == stage) for i in range(8)]
    pairs = []
    for x in range(4):
        for y in range(4):
            for z in range(8):
                for c in range(2):
                    to = moved(x, y, z, c, bits)
                    pairs.append((x * 64 + y * 16 + z * 2 + c, to[0] * 64 + to[1] * 16 + to[2] * 2 + to[3]))
    return pairs


def row_order():
    dp, space = lax.axis_index("dp"), lax.axis_index("space")
    place = lax.iota(jnp.int32, COUT)
    bits = [place >> (7 - i) & 1 for i in range(8)]
    x, y, z, c = moved(dp // 4, dp % 4, space // 2, space % 2, bits)
    row = x * 64 + y * 16 + z * 2 + c
    return (row[:, None] == lax.iota(jnp.int32, COUT)[None, :]).astype(bf16)


def together(*arrays):
    return lax.optimization_barrier(arrays)


def swapped(send, stage):
    return lax.ppermute(send, ("dp", "space"), partners(stage))


def halved(keep, received, stage):
    total = keep + received.astype(f32)
    half = total.shape[0] // 2
    return total[:half], total[half:].astype(bf16 if stage < 5 else f32)


def shards(volume, weight, cotangent):
    volume = volume.reshape(SLAB, CELLS, CIN)
    cot = cotangent.reshape(SLAB * CELLS, COUT)
    weight = weight.reshape(TAPS * CIN, COUT)
    before, after = neighbours(volume[SLAB - 1], 1), neighbours(volume[0], -1)
    cot, before, after = together(cot, before, after)
    cot_before = neighbours(cot[(SLAB - 1) * CELLS :], 1)
    cot_after = neighbours(cot[:CELLS], -1)
    keep, send = weight_grad_share(row_order(), before, volume, after, cot)
    send, cot_before, cot_after = together(send, cot_before, cot_after)
    keep, send = halved(keep, swapped(send, 0), 0)

    received = swapped(send, 1)
    forward_weight, send = together(weight, send)
    activation = forward(before, volume, after, forward_weight)
    received, activation = together(received, activation)
    keep, send = halved(keep, received, 1)
    received = swapped(send, 2)
    back_weight, send = together(weight, send)
    input_grad = input_grad_of(cot_before, cot, cot_after, back_weight)
    received, input_grad = together(received, input_grad)

    for stage in range(2, 7):
        keep, send = halved(keep, received, stage)
        received = swapped(send, stage + 1)
    total = keep + received
    count = lax.axis_size("dp") * lax.axis_size("space") * SLAB * CELLS
    return (
        activation.reshape(1, SLAB, SIDE, SIDE, COUT),
        input_grad.reshape(1, SLAB, SIDE, SIDE, CIN),
        total / jnp.sqrt(f32(count)),
    )


def solution(mesh):
    slabs = P("dp", "space", None, None, None)
    return jax.shard_map(
        shards,
        mesh=mesh,
        in_specs=(slabs, P(), slabs),
        out_specs=(slabs, slabs, P(("dp", "space"), None)),
        check_vma=False,
    )
```

time: 363 us -> 80.3 us (0.22)
  waiting for transfers between devices: 260 us -> 19.8 us
  matrix products: 37.1 us -> 0 us
  local copies, waits for them, and re-layouts: 32.2 us -> 1.76 us
  starting transfers between devices: 9.96 us -> 37.3 us
  Pallas kernels: 0 us -> 19.3 us
  between operations: 14.6 us -> 0.85 us
  other arithmetic: 7.91 us -> 1.09 us
    unnamed x2 -> x0, waiting for transfers between devices: 260 us -> none
    dot_general x47 -> x0, matrix products: 37.1 us -> none  [the longest x27 14.2 us: shards(): lax.dot_general(shifted, weight[k], contract_out, preferred_element_type=...]
    ppermute x4 -> x12, starting transfers between devices: 9.92 us -> 37.3 us  [the longest x8 25.6 us: swapped(): return lax.ppermute(send, ('dp', 'space'), partners(stage))]
    ppermute x4 -> x12, waiting for transfers between devices: 0.01 us -> 19.8 us  [the longest x8 16.1 us: swapped(): return lax.ppermute(send, ('dp', 'space'), partners(stage))]
    slice x6 -> x9, local copies, waits for them, and re-layouts: 20.9 us -> 1.4 us  [the longest x1 1.18 us: shards(): before, after = (neighbours(volume[SLAB - 1], 1), neighbours(volume[0], -1))]
    pallas_call x0 -> x3, Pallas kernels: none -> 19.3 us  [call(): pl.pallas_call(kernel, out_shape=outs, in_specs=[in_vmem()] * len(args),...]
    unnamed x49 -> x6, local copies, waits for them, and re-layouts: 11.1 us -> 0.36 us
  transfers between devices with their start and end apart: 5 -> 12, of which waited for: 1 -> 8; matrix products, arithmetic and copies ran while one was open for 16% -> 0% of each run, Pallas kernels for 0% -> 24%
where the time goes in v1:
time: 80.3 us; the launch traced here: 80.1 us
  starting transfers between devices  37.3 us (46%)
  waiting for transfers between devices  19.8 us (25%)
  Pallas kernels  19.3 us (24%)
  local copies, waits for them, and re-layouts  1.76 us (2%)
  other arithmetic  1.09 us (1%)
  between operations  0.85 us (1%)
    ppermute x8, starting transfers between devices, swapped(): return lax.ppermute(send, ('dp', 'space'), partners(stage))  25.6 us
    pallas_call x3, Pallas kernels, call(): pl.pallas_call(kernel, out_shape=outs, in_specs=[in_vmem()] * len(args),...  19.3 us
    ppermute x8, waiting for transfers between devices, swapped(): return lax.ppermute(send, ('dp', 'space'), partners(stage))  16.1 us
    ppermute x4, starting transfers between devices, neighbours(): return lax.ppermute(value, 'space', pairs)  11.7 us
    ppermute x4, waiting for transfers between devices, neighbours(): return lax.ppermute(value, 'space', pairs)  3.76 us
  transfers between devices with their start and end apart: 12, of which 8 were waited for; matrix products, arithmetic and copies ran while one was open for 0% of the time, Pallas kernels for 24%

profile of v1, /device:TPU:6, one launch (start us, length us, event | category | flops | bytes accessed | tf_op | source)
XLA Modules:
  0.0 80.1 jit_solution(9689474188065019500)
XLA Ops:
  0.6 1.2 %fusion.22 = (bf16[1,1,32,32,128]{4,3,2,1,0:T(8,128)(2,1)S(1)}, bf16[1,1,32,32,128]{4,3,2,1,0:T(8,128)(2,1)S(1)}) fusion(bf16[1,2,32,32,128]{4,3,2,1,0:T(8,128)(2,1)} %param.3), kind=kLoop, calls=%fused_computation.43 | loop fusion | bytes 1048576 | tf_op jit(solution)/shard_map/slice | solution.py:217
  1.8 1.8 %collective-permute-start = (bf16[1024,128]{1,0:T(8,128)(2,1)S(1)}, bf16[1024,128]{1,0:T(8,128)(2,1)S(1)}, u32[]{:S(2)}, u32[]{:S(2)}) collective-permute-start(bf16[1024,128]{1,0:T(8,128)(2,1)S(1)} %bitcast.15), channel_id=1, source_target_pairs={{0,1},{1,2},{2,3},{3,4},{4,5},{5,6},{6,7},{7,8},{8,9},{9,10},{10,1... | collective-permute-start | bytes 786440 | tf_op jit(solution)/shard_map/ppermute | solution.py:166
  3.6 1.3 %collective-permute-start.1 = (bf16[1024,128]{1,0:T(8,128)(2,1)S(1)}, bf16[1024,128]{1,0:T(8,128)(2,1)S(1)}, u32[]{:S(2)}, u32[]{:S(2)}) collective-permute-start(bf16[1024,128]{1,0:T(8,128)(2,1)S(1)} %bitcast.14), channel_id=1, source_target_pairs={{1,0},{2,1},{3,2},{4,3},{5,4},{6,5},{7,6},{8,7},{9,8},{10,9},{11,1... | collective-permute-start | bytes 786440 | tf_op jit(solution)/shard_map/ppermute | solution.py:166
  5.0 3.8 %collective-permute-done.1.after = bf16[1024,128]{1,0:T(8,128)(2,1)S(1)} collective-permute-done((bf16[1024,128]{1,0:T(8,128)(2,1)S(1)}, bf16[1024,128]{1,0:T(8,128)(2,1)S(1)}, u32[]{:S(2)}, u32[]{:S(2)}) %collective-permute-start.1) | collective-permute-done | bytes 262176 | tf_op jit(solution)/shard_map/ppermute | solution.py:166
  8.7 0.1 fusion.21
  8.8 1.3 %collective-permute-start.3 = (bf16[1024,256]{1,0:T(8,128)(2,1)S(1)}, bf16[1024,256]{1,0:T(8,128)(2,1)S(1)}, u32[]{:S(2)}, u32[]{:S(2)}) collective-permute-start(bf16[1024,256]{1,0:T(8,128)(2,1)S(1)} %get-tuple-element.31), channel_id=1, source_target_pairs={{1,0},{2,1},{3,2},{4,3},{5,4},{6,5},{7,6},{8,7},{9,8},{10,9},{11,1... | collective-permute-start | bytes 1572872 | tf_op jit(solution)/shard_map/ppermute | solution.py:166
  10.1 7.3 %collective-permute-start.2 = (bf16[1024,256]{1,0:T(8,128)(2,1)S(1)}, bf16[1024,256]{1,0:T(8,128)(2,1)S(1)}, u32[]{:S(2)}, u32[]{:S(2)}) collective-permute-start(bf16[1024,256]{1,0:T(8,128)(2,1)S(1)} %get-tuple-element.32), channel_id=1, source_target_pairs={{0,1},{1,2},{2,3},{3,4},{4,5},{5,6},{6,7},{7,8},{8,9},{9,10},{10,1... | collective-permute-start | bytes 1572872 | tf_op jit(solution)/shard_map/ppermute | solution.py:166
  17.4 0.1 fusion.order
  17.5 4.6 %weight_grad.1 = (f32[128,3456]{1,0:T(8,128)S(1)}, bf16[128,3456]{1,0:T(8,128)(2,1)S(1)}) custom-call(bf16[256,256]{1,0:T(8,128)(2,1)S(1)} %fusion.order, bf16[1024,128]{1,0:T(8,128)(2,1)S(1)} %collective-permute-done.before, bf16[2,1024,128]{2,1,0:T(8,128)(2,1)S(1)} %bitcast.10, bf16[1024,128]{1,0:T(8,128)(2,1)S(1)} %collective-permute-done.1.after, ...), custom_call_target="tpu_custom_call" | custom-call | flops 3623878656 | bytes 5242880 | tf_op jit(solution)/shard_map/weight_grad/pallas_call | solution.py:25
  22.2 3.0 %collective-permute-start.4 = (bf16[128,3456]{1,0:T(8,128)(2,1)S(1)}, bf16[128,3456]{1,0:T(8,128)(2,1)S(1)}, u32[]{:S(2)}, u32[]{:S(2)}) collective-permute-start(bf16[128,3456]{1,0:T(8,128)(2,1)S(1)} %get-tuple-element.22), channel_id=1, source_target_pairs={{0,1},{1,0},{2,3},{3,2},{4,5},{5,4},{6,7},{7,6},{8,9},{9,8},{10,11... | collective-permute-start | bytes 2654216 | tf_op jit(solution)/shard_map/ppermute | solution.py:204
  25.2 2.1 %collective-permute-done.4 = bf16[128,3456]{1,0:T(8,128)(2,1)S(1)} collective-permute-done((bf16[128,3456]{1,0:T(8,128)(2,1)S(1)}, bf16[128,3456]{1,0:T(8,128)(2,1)S(1)}, u32[]{:S(2)}, u32[]{:S(2)}) %collective-permute-start.4) | collective-permute-done | bytes 884768 | tf_op jit(solution)/shard_map/ppermute | solution.py:204
  27.3 0.1 convert_add_fusion
  27.4 0.1 slice.107
  27.5 0.9 %collective-permute-start.5 = (bf16[64,3456]{1,0:T(8,128)(2,1)S(1)}, bf16[64,3456]{1,0:T(8,128)(2,1)S(1)}, u32[]{:S(2)}, u32[]{:S(2)}) collective-permute-start(bf16[64,3456]{1,0:T(8,128)(2,1)S(1)} %slice.107), channel_id=1, source_target_pairs={{0,64},{1,17},{2,66},{3,19},{4,68},{5,21},{6,70},{7,23},{8,72},{9,... | collective-permute-start | bytes 1327112 | tf_op jit(solution)/shard_map/ppermute | solution.py:204
  28.4 0.4 copy-done.2
  28.8 7.0 %forward.1 = bf16[2048,256]{1,0:T(8,128)(2,1)} custom-call(bf16[1024,128]{1,0:T(8,128)(2,1)S(1)} %collective-permute-done.before, bf16[2,1024,128]{2,1,0:T(8,128)(2,1)S(1)} %bitcast.11, bf16[1024,128]{1,0:T(8,128)(2,1)S(1)} %collective-permute-done.1.after, bf16[3456,256]{1,0:T(8,128)(2,1)S(1)} %bitcast.12), custom_call_target="tpu_custom_call" | custom-call | flops 3623878656 | bytes 5242880 | tf_op jit(solution)/shard_map/forward/pallas_call | solution.py:25
  35.7 0.1 collective-permute-done.5
  35.9 0.1 slice_add_fusion
  36.0 1.7 %collective-permute-start.6 = (bf16[32,3456]{1,0:T(8,128)(2,1)S(1)}, bf16[32,3456]{1,0:T(8,128)(2,1)S(1)}, u32[]{:S(2)}, u32[]{:S(2)}) collective-permute-start(bf16[32,3456]{1,0:T(8,128)(2,1)S(1)} %slice.108), channel_id=1, source_target_pairs={{0,16},{1,65},{2,18},{3,67},{4,20},{5,69},{6,22},{7,71},{8,24},{9,... | collective-permute-start | bytes 663560 | tf_op jit(solution)/shard_map/ppermute | solution.py:204
  37.7 7.7 %input_grad.1 = bf16[2048,128]{1,0:T(8,128)(2,1)} custom-call(bf16[1024,256]{1,0:T(8,128)(2,1)S(1)} %collective-permute-done.2.before, bf16[2048,256]{1,0:T(8,128)(2,1)S(1)} %bitcast.9, bf16[1024,256]{1,0:T(8,128)(2,1)S(1)} %collective-permute-done.3.after, bf16[3456,256]{1,0:T(8,128)(2,1)S(1)} %bitcast.13), custom_call_target="tpu_custom_call" | custom-call | flops 3623878656 | bytes 5242880 | tf_op jit(solution)/shard_map/input_grad/pallas_call | solution.py:25
  45.3 0.1 slice_add_fusion.1
  45.4 0.7 collective-permute-start.7
  46.2 5.3 %collective-permute-done.7 = bf16[16,3456]{1,0:T(8,128)(2,1)S(1)} collective-permute-done((bf16[16,3456]{1,0:T(8,128)(2,1)S(1)}, bf16[16,3456]{1,0:T(8,128)(2,1)S(1)}, u32[]{:S(2)}, u32[]{:S(2)}) %collective-permute-start.7) | collective-permute-done | bytes 110624 | tf_op jit(solution)/shard_map/ppermute | solution.py:204
  51.5 2.3 %collective-permute-start.8 = (bf16[8,3456]{1,0:T(8,128)(2,1)S(1)}, bf16[8,3456]{1,0:T(8,128)(2,1)S(1)}, u32[]{:S(2)}, u32[]{:S(2)}) collective-permute-start(bf16[8,3456]{1,0:T(8,128)(2,1)S(1)} %slice.110), channel_id=1, source_target_pairs={{0,48},{1,193},{2,50},{3,195},{4,52},{5,197},{6,54},{7,199},{8,56}... | collective-permute-start | bytes 165896 | tf_op jit(solution)/shard_map/ppermute | solution.py:204
  53.8 3.2 %collective-permute-done.8 = bf16[8,3456]{1,0:T(8,128)(2,1)S(1)} collective-permute-done((bf16[8,3456]{1,0:T(8,128)(2,1)S(1)}, bf16[8,3456]{1,0:T(8,128)(2,1)S(1)}, u32[]{:S(2)}, u32[]{:S(2)}) %collective-permute-start.8) | collective-permute-done | bytes 55328 | tf_op jit(solution)/shard_map/ppermute | solution.py:204
  57.0 2.8 %collective-permute-start.9 = (bf16[4,3456]{1,0:T(4,128)(2,1)S(1)}, bf16[4,3456]{1,0:T(4,128)(2,1)S(1)}, u32[]{:S(2)}, u32[]{:S(2)}) collective-permute-start(bf16[4,3456]{1,0:T(4,128)(2,1)S(1)} %slice.111), channel_id=1, source_target_pairs={{0,2},{1,3},{2,0},{3,1},{4,6},{5,7},{6,4},{7,5},{8,10},{9,11},{10,... | collective-permute-start | bytes 82952 | tf_op jit(solution)/shard_map/ppermute | solution.py:204
  59.8 1.8 %collective-permute-done.9 = bf16[4,3456]{1,0:T(4,128)(2,1)S(1)} collective-permute-done((bf16[4,3456]{1,0:T(4,128)(2,1)S(1)}, bf16[4,3456]{1,0:T(4,128)(2,1)S(1)}, u32[]{:S(2)}, u32[]{:S(2)}) %collective-permute-start.9) | collective-permute-done | bytes 27680 | tf_op jit(solution)/shard_map/ppermute | solution.py:204
  61.7 6.2 %collective-permute-start.10 = (f32[2,3456]{1,0:T(2,128)S(1)}, f32[2,3456]{1,0:T(2,128)S(1)}, u32[]{:S(2)}, u32[]{:S(2)}) collective-permute-start(f32[2,3456]{1,0:T(2,128)S(1)} %slice.90), channel_id=1, source_target_pairs={{0,4},{1,5},{2,6},{3,7},{4,0},{5,1},{6,2},{7,3},{8,12},{9,13},{10,... | collective-permute-start | bytes 82952 | tf_op jit(solution)/shard_map/ppermute | solution.py:204
  67.9 1.8 %collective-permute-done.10 = f32[2,3456]{1,0:T(2,128)S(1)} collective-permute-done((f32[2,3456]{1,0:T(2,128)S(1)}, f32[2,3456]{1,0:T(2,128)S(1)}, u32[]{:S(2)}, u32[]{:S(2)}) %collective-permute-start.10) | collective-permute-done | bytes 27680 | tf_op jit(solution)/shard_map/ppermute | solution.py:204
  69.8 8.0 %collective-permute-start.11 = (f32[1,3456]{1,0:T(1,128)S(1)}, f32[1,3456]{1,0:T(1,128)S(1)}, u32[]{:S(2)}, u32[]{:S(2)}) collective-permute-start(f32[1,3456]{1,0:T(1,128)S(1)} %slice.92), channel_id=1, source_target_pairs={{0,8},{1,9},{2,10},{3,11},{4,12},{5,13},{6,14},{7,15},{8,0},{9,1},... | collective-permute-start | bytes 41480 | tf_op jit(solution)/shard_map/ppermute | solution.py:204
  77.8 1.7 %collective-permute-done.11 = f32[1,3456]{1,0:T(1,128)S(1)} collective-permute-done((f32[1,3456]{1,0:T(1,128)S(1)}, f32[1,3456]{1,0:T(1,128)S(1)}, u32[]{:S(2)}, u32[]{:S(2)}) %collective-permute-start.11) | collective-permute-done | bytes 13856 | tf_op jit(solution)/shard_map/ppermute | solution.py:204
  79.5 0.6 fusion.1
  (20 shorter events, 0.2 us)
Async XLA Ops:
  0.6 8.1 %copy-start = (bf16[1,2,32,32,256]{4,3,2,1,0:T(8,128)(2,1)S(1)}, bf16[1,2,32,32,256]{4,3,2,1,0:T(8,128)(2,1)}, u32[]{:S(2)}) copy-start(bf16[1,2,32,32,256]{4,3,2,1,0:T(8,128)(2,1)} %param.5) | copy-start | bytes 3145732
  0.6 16.9 %copy-start.1 = (bf16[1,2,32,32,128]{4,3,2,1,0:T(8,128)(2,1)S(1)}, bf16[1,2,32,32,128]{4,3,2,1,0:T(8,128)(2,1)}, u32[]{:S(2)}) copy-start(bf16[1,2,32,32,128]{4,3,2,1,0:T(8,128)(2,1)} %param.3) | copy-start | bytes 1572868
  1.8 3.1 %collective-permute-start = (bf16[1024,128]{1,0:T(8,128)(2,1)S(1)}, bf16[1024,128]{1,0:T(8,128)(2,1)S(1)}, u32[]{:S(2)}, u32[]{:S(2)}) collective-permute-start(bf16[1024,128]{1,0:T(8,128)(2,1)S(1)} %bitcast.15), channel_id=1, source_target_pairs={{0,1},{1,2},{2,3},{3,4},{4,5},{5,6},{6,7},{7,8},{8,9},{9,10},{10,1... | collective-permute-start | bytes 786440 | tf_op jit(solution)/shard_map/ppermute | solution.py:166
  3.6 5.1 %collective-permute-start.1 = (bf16[1024,128]{1,0:T(8,128)(2,1)S(1)}, bf16[1024,128]{1,0:T(8,128)(2,1)S(1)}, u32[]{:S(2)}, u32[]{:S(2)}) collective-permute-start(bf16[1024,128]{1,0:T(8,128)(2,1)S(1)} %bitcast.14), channel_id=1, source_target_pairs={{1,0},{2,1},{3,2},{4,3},{5,4},{6,5},{7,6},{8,7},{9,8},{10,9},{11,1... | collective-permute-start | bytes 786440 | tf_op jit(solution)/shard_map/ppermute | solution.py:166
  8.8 13.4 %collective-permute-start.3 = (bf16[1024,256]{1,0:T(8,128)(2,1)S(1)}, bf16[1024,256]{1,0:T(8,128)(2,1)S(1)}, u32[]{:S(2)}, u32[]{:S(2)}) collective-permute-start(bf16[1024,256]{1,0:T(8,128)(2,1)S(1)} %get-tuple-element.31), channel_id=1, source_target_pairs={{1,0},{2,1},{3,2},{4,3},{5,4},{6,5},{7,6},{8,7},{9,8},{10,9},{11,1... | collective-permute-start | bytes 1572872 | tf_op jit(solution)/shard_map/ppermute | solution.py:166
  10.1 12.1 %collective-permute-start.2 = (bf16[1024,256]{1,0:T(8,128)(2,1)S(1)}, bf16[1024,256]{1,0:T(8,128)(2,1)S(1)}, u32[]{:S(2)}, u32[]{:S(2)}) collective-permute-start(bf16[1024,256]{1,0:T(8,128)(2,1)S(1)} %get-tuple-element.32), channel_id=1, source_target_pairs={{0,1},{1,2},{2,3},{3,4},{4,5},{5,6},{6,7},{7,8},{8,9},{9,10},{10,1... | collective-permute-start | bytes 1572872 | tf_op jit(solution)/shard_map/ppermute | solution.py:166
  22.2 5.1 %collective-permute-start.4 = (bf16[128,3456]{1,0:T(8,128)(2,1)S(1)}, bf16[128,3456]{1,0:T(8,128)(2,1)S(1)}, u32[]{:S(2)}, u32[]{:S(2)}) collective-permute-start(bf16[128,3456]{1,0:T(8,128)(2,1)S(1)} %get-tuple-element.22), channel_id=1, source_target_pairs={{0,1},{1,0},{2,3},{3,2},{4,5},{5,4},{6,7},{7,6},{8,9},{9,8},{10,11... | collective-permute-start | bytes 2654216 | tf_op jit(solution)/shard_map/ppermute | solution.py:204
  27.3 1.5 %copy-start.2 = (bf16[27,128,256]{2,1,0:T(8,128)(2,1)S(1)}, bf16[27,128,256]{2,1,0:T(8,128)(2,1)}, u32[]{:S(2)}) copy-start(bf16[27,128,256]{2,1,0:T(8,128)(2,1)} %param.4) | copy-start | bytes 5308420
  27.5 8.4 %collective-permute-start.5 = (bf16[64,3456]{1,0:T(8,128)(2,1)S(1)}, bf16[64,3456]{1,0:T(8,128)(2,1)S(1)}, u32[]{:S(2)}, u32[]{:S(2)}) collective-permute-start(bf16[64,3456]{1,0:T(8,128)(2,1)S(1)} %slice.107), channel_id=1, source_target_pairs={{0,64},{1,17},{2,66},{3,19},{4,68},{5,21},{6,70},{7,23},{8,72},{9,... | collective-permute-start | bytes 1327112 | tf_op jit(solution)/shard_map/ppermute | solution.py:204
  36.0 9.3 %collective-permute-start.6 = (bf16[32,3456]{1,0:T(8,128)(2,1)S(1)}, bf16[32,3456]{1,0:T(8,128)(2,1)S(1)}, u32[]{:S(2)}, u32[]{:S(2)}) collective-permute-start(bf16[32,3456]{1,0:T(8,128)(2,1)S(1)} %slice.108), channel_id=1, source_target_pairs={{0,16},{1,65},{2,18},{3,67},{4,20},{5,69},{6,22},{7,71},{8,24},{9,... | collective-permute-start | bytes 663560 | tf_op jit(solution)/shard_map/ppermute | solution.py:204
  45.4 6.0 %collective-permute-start.7 = (bf16[16,3456]{1,0:T(8,128)(2,1)S(1)}, bf16[16,3456]{1,0:T(8,128)(2,1)S(1)}, u32[]{:S(2)}, u32[]{:S(2)}) collective-permute-start(bf16[16,3456]{1,0:T(8,128)(2,1)S(1)} %slice.109), channel_id=1, source_target_pairs={{0,192},{1,49},{2,194},{3,51},{4,196},{5,53},{6,198},{7,55},{8,200... | collective-permute-start | bytes 331784 | tf_op jit(solution)/shard_map/ppermute | solution.py:204
  51.5 5.5 %collective-permute-start.8 = (bf16[8,3456]{1,0:T(8,128)(2,1)S(1)}, bf16[8,3456]{1,0:T(8,128)(2,1)S(1)}, u32[]{:S(2)}, u32[]{:S(2)}) collective-permute-start(bf16[8,3456]{1,0:T(8,128)(2,1)S(1)} %slice.110), channel_id=1, source_target_pairs={{0,48},{1,193},{2,50},{3,195},{4,52},{5,197},{6,54},{7,199},{8,56}... | collective-permute-start | bytes 165896 | tf_op jit(solution)/shard_map/ppermute | solution.py:204
  57.0 4.7 %collective-permute-start.9 = (bf16[4,3456]{1,0:T(4,128)(2,1)S(1)}, bf16[4,3456]{1,0:T(4,128)(2,1)S(1)}, u32[]{:S(2)}, u32[]{:S(2)}) collective-permute-start(bf16[4,3456]{1,0:T(4,128)(2,1)S(1)} %slice.111), channel_id=1, source_target_pairs={{0,2},{1,3},{2,0},{3,1},{4,6},{5,7},{6,4},{7,5},{8,10},{9,11},{10,... | collective-permute-start | bytes 82952 | tf_op jit(solution)/shard_map/ppermute | solution.py:204
  61.7 8.0 %collective-permute-start.10 = (f32[2,3456]{1,0:T(2,128)S(1)}, f32[2,3456]{1,0:T(2,128)S(1)}, u32[]{:S(2)}, u32[]{:S(2)}) collective-permute-start(f32[2,3456]{1,0:T(2,128)S(1)} %slice.90), channel_id=1, source_target_pairs={{0,4},{1,5},{2,6},{3,7},{4,0},{5,1},{6,2},{7,3},{8,12},{9,13},{10,... | collective-permute-start | bytes 82952 | tf_op jit(solution)/shard_map/ppermute | solution.py:204
  69.8 9.7 %collective-permute-start.11 = (f32[1,3456]{1,0:T(1,128)S(1)}, f32[1,3456]{1,0:T(1,128)S(1)}, u32[]{:S(2)}, u32[]{:S(2)}) collective-permute-start(f32[1,3456]{1,0:T(1,128)S(1)} %slice.92), channel_id=1, source_target_pairs={{0,8},{1,9},{2,10},{3,11},{4,12},{5,13},{6,14},{7,15},{8,0},{9,1},... | collective-permute-start | bytes 41480 | tf_op jit(solution)/shard_map/ppermute | solution.py:204

commit v2 on v1

v2 whole, which is shorter than its diff:
```python
import jax
import jax.numpy as jnp
from jax import lax
from jax.experimental import pallas as pl
from jax.experimental.pallas import tpu as pltpu
from jax.sharding import PartitionSpec as P

bf16, f32 = jnp.bfloat16, jnp.float32
SIDE = 32
CELLS = SIDE * SIDE
CIN, COUT, TAPS = 128, 256, 27
SLAB = 2
PADDED = CELLS + 2 * SIDE
ROWS = 1024
VMEM_LIMIT = 24 << 20
FLOPS = 2 * SLAB * CELLS * TAPS * CIN * COUT


def in_vmem():
    return pl.BlockSpec(memory_space=pltpu.VMEM)


def call(kernel, name, outs, scratch, args, flops):
    return pl.pallas_call(
        kernel,
        out_shape=outs,
        in_specs=[in_vmem()] * len(args),
        out_specs=tuple(in_vmem() for _ in outs),
        scratch_shapes=scratch,
        compiler_params=pltpu.CompilerParams(vmem_limit_bytes=VMEM_LIMIT),
        cost_estimate=pl.CostEstimate(flops=flops, bytes_accessed=4 << 20, transcendentals=0),
        name=name,
    )(*args)


def call_for_plane(kernel, name, d, lanes, scratch, args, earlier, flops):
    specs = [in_vmem()] * len(args)
    aliases = {}
    if earlier is not None:
        aliases = {len(args): 0}
        args, specs = (*args, earlier), specs + [pl.BlockSpec(memory_space=pl.ANY)]
    return pl.pallas_call(
        kernel,
        out_shape=jax.ShapeDtypeStruct((SLAB * CELLS, lanes), bf16),
        grid=(1,),
        in_specs=specs,
        out_specs=pl.BlockSpec((CELLS, lanes), lambda i: (d, 0)),
        scratch_shapes=scratch,
        input_output_aliases=aliases,
        compiler_params=pltpu.CompilerParams(vmem_limit_bytes=VMEM_LIMIT),
        cost_estimate=pl.CostEstimate(flops=flops, bytes_accessed=4 << 20, transcendentals=0),
        name=name,
    )(*args)


def product(a, b):
    return jnp.dot(a, b, preferred_element_type=f32)


def fill_taps(planes, wide, taps):
    col = lax.broadcasted_iota(jnp.int32, (CELLS, CIN), 0) % SIDE
    zero = jnp.zeros((SIDE, 3 * CIN), bf16)
    inner = pl.ds(SIDE, CELLS)
    for i, plane in enumerate(planes):
        wide[pl.ds(8, CELLS), :] = plane[...].astype(f32)
        taps[i, pl.ds(0, SIDE), :] = zero
        taps[i, pl.ds(SIDE + CELLS, SIDE), :] = zero
        left = jnp.where(col > 0, wide[pl.ds(7, CELLS), :], 0.0)
        right = jnp.where(col < SIDE - 1, wide[pl.ds(9, CELLS), :], 0.0)
        taps[i, inner, pl.ds(0, CIN)] = left.astype(bf16)
        taps[i, inner, pl.ds(CIN, CIN)] = plane[...]
        taps[i, inner, pl.ds(2 * CIN, CIN)] = right.astype(bf16)


WIDE = pltpu.VMEM((CELLS + 16, CIN), f32)
TAP_PLANES = jax.ShapeDtypeStruct((2, PADDED, 3 * CIN), bf16)


def taps_at(taps, plane, some):
    parts = [taps[plane, pl.ds(k // 3 % 3 * SIDE, CELLS), pl.ds(k % 3 * CIN, CIN)] for k in some]
    return jnp.concatenate(parts, axis=1)


def tap_groups(kd):
    return [range(k, min(k + 2, 9 * kd + 9)) for k in range(9 * kd, 9 * kd + 9, 2)]


def local_share_kernel(order, volume, cot, taps, turned, share, wide):
    fill_taps((volume.at[0], volume.at[1]), wide, taps)
    for j in range(SLAB * CELLS // 256):
        rows = pl.ds(j * 256, 256)
        turned[:, rows] = lax.dot_general(
            order[...], cot[rows, :], (((1,), (1,)), ((), ())), preferred_element_type=f32
        ).astype(bf16)
    for kd in range(3):
        for some in tap_groups(kd):
            total = None
            for d in range(SLAB):
                if 0 <= d + kd - 1 < SLAB:
                    part = product(turned[:, pl.ds(d * CELLS, CELLS)], taps_at(taps, d + kd - 1, some))
                    total = part if total is None else total + part
            share[:, pl.ds(some[0] * CIN, len(some) * CIN)] = total


def local_share(order, volume, cot):
    return call(
        local_share_kernel,
        "local_share",
        (
            TAP_PLANES,
            jax.ShapeDtypeStruct((COUT, SLAB * CELLS), bf16),
            jax.ShapeDtypeStruct((COUT, TAPS * CIN), f32),
        ),
        [WIDE],
        (order, volume, cot),
        FLOPS * 2 // 3,
    )


def edge_share_kernel(before, after, turned, share, taps, keep, send, wide):
    fill_taps((before, after), wide, taps)
    for kd in range(3):
        for some in tap_groups(kd):
            lanes = pl.ds(some[0] * CIN, len(some) * CIN)
            total = share[:, lanes]
            if kd != 1:
                edge = kd // 2
                total = total + product(turned[:, pl.ds(edge * CELLS, CELLS)], taps_at(taps, edge, some))
            keep[:, lanes] = total[: COUT // 2]
            send[:, lanes] = total[COUT // 2 :].astype(bf16)


def edge_share(before, after, turned, share):
    half = (COUT // 2, TAPS * CIN)
    return call(
        edge_share_kernel,
        "edge_share",
        (TAP_PLANES, jax.ShapeDtypeStruct(half, f32), jax.ShapeDtypeStruct(half, bf16)),
        [WIDE],
        (before, after, turned, share),
        FLOPS // 3,
    )


def forward(d, inner, outer, weight, earlier):
    def kernel(inner, outer, weight, *rest):
        out = rest[-1]
        planes = [(outer, 0), (inner, 0), (inner, 1), (outer, 1)][d : d + 3]

        def step(i, carry):
            base = pl.multiple_of(i * ROWS, ROWS)
            parts = []
            for k in range(TAPS):
                taps, plane = planes[k // 9]
                rows = pl.ds(pl.multiple_of(base + k // 3 % 3 * SIDE, SIDE), ROWS)
                parts.append(taps[plane, rows, pl.ds(k % 3 * CIN, CIN)])
            pre = product(jnp.concatenate(parts, axis=1), weight[...])
            out[pl.ds(base, ROWS), :] = jnp.where(pre >= 0, pre, 0.3 * pre).astype(bf16)
            return carry

        lax.fori_loop(0, CELLS // ROWS, step, 0)

    name = "forward_%d" % d
    return call_for_plane(kernel, name, d, COUT, [], (inner, outer, weight), earlier, FLOPS // 2)


def turn_weight_kernel(weight, turned):
    for k in range(TAPS):
        turned[pl.ds(k // 3 * COUT, COUT), pl.ds(k % 3 * CIN, CIN)] = weight[pl.ds(k * CIN, CIN), :].T


def turn_weight(weight):
    shape = jax.ShapeDtypeStruct((9 * COUT, 3 * CIN), bf16)
    return call(turn_weight_kernel, "turn_weight", (shape,), [], (weight,), 1 << 20)[0]


def input_grad_plane(d, before, cot, after, turned, earlier):
    def kernel(before, cot, after, turned, *rest):
        out, padded, sums = rest[-3:]
        zero = jnp.zeros((SIDE, COUT), bf16)
        planes = (before, cot.at[pl.ds(0, CELLS)], cot.at[pl.ds(CELLS, CELLS)], after)[d : d + 3]
        for i, plane in enumerate(planes):
            padded[i, pl.ds(0, SIDE), :] = zero
            padded[i, pl.ds(SIDE + CELLS, SIDE), :] = zero
            padded[i, pl.ds(SIDE, CELLS), :] = plane[...]
        col = lax.broadcasted_iota(jnp.int32, (ROWS, CIN), 0) % SIDE

        def step(i, carry):
            base = pl.multiple_of(i * ROWS, ROWS)
            parts = [
                padded[2 - j // 3, pl.ds(pl.multiple_of(base + (2 - j % 3) * SIDE, SIDE), ROWS), :]
                for j in range(9)
            ]
            sums[pl.ds(8, ROWS), :] = product(jnp.concatenate(parts, axis=1), turned[...])
            total = sums[pl.ds(8, ROWS), pl.ds(CIN, CIN)]
            total = total + jnp.where(col < SIDE - 1, sums[pl.ds(9, ROWS), pl.ds(0, CIN)], 0.0)
            total = total + jnp.where(col > 0, sums[pl.ds(7, ROWS), pl.ds(2 * CIN, CIN)], 0.0)
            out[pl.ds(base, ROWS), :] = total.astype(bf16)
            return carry

        lax.fori_loop(0, CELLS // ROWS, step, 0)

    scratch = [pltpu.VMEM((3, PADDED, COUT), bf16), pltpu.VMEM((ROWS + 16, 3 * CIN), f32)]
    name = "input_grad_%d" % d
    return call_for_plane(kernel, name, d, CIN, scratch, (before, cot, after, turned), earlier, FLOPS // 2)


def neighbours(value, step):
    pairs = [(i, i + step) for i in range(16) if 0 <= i + step < 16]
    return lax.ppermute(value, "space", pairs)


def moved(x, y, z, c, bits):
    b = bits
    c = c ^ b[0]
    first, second = b[1] ^ (3 * b[3]), b[2] ^ (3 * b[4])
    x = x ^ (first + (second - first) * c)
    y = y ^ (second + (first - second) * c)
    even = lambda z: z ^ 1
    odd = lambda z: ((z + 1) % 8 ^ 1) + 7 & 7
    z = z + (even(z) - z) * b[5]
    z = z + (odd(z) - z) * b[6]
    z = z + (even(odd(even(z))) - z) * b[7]
    return x, y, z, c


def partners(stage):
    bits = [int(i == stage) for i in range(8)]
    pairs = []
    for x in range(4):
        for y in range(4):
            for z in range(8):
                for c in range(2):
                    to = moved(x, y, z, c, bits)
                    pairs.append((x * 64 + y * 16 + z * 2 + c, to[0] * 64 + to[1] * 16 + to[2] * 2 + to[3]))
    return pairs


def row_order():
    dp, space = lax.axis_index("dp"), lax.axis_index("space")
    place = lax.iota(jnp.int32, COUT)
    bits = [place >> (7 - i) & 1 for i in range(8)]
    x, y, z, c = moved(dp // 4, dp % 4, space // 2, space % 2, bits)
    row = x * 64 + y * 16 + z * 2 + c
    return (row[:, None] == lax.iota(jnp.int32, COUT)[None, :]).astype(bf16)


def together(*arrays):
    return lax.optimization_barrier(arrays)


def swapped(send, stage):
    return lax.ppermute(send, ("dp", "space"), partners(stage))


def halved(keep, received, stage):
    total = keep + received.astype(f32)
    half = total.shape[0] // 2
    return total[:half], total[half:].astype(bf16 if stage < 5 else f32)


def shards(volume, weight, cotangent):
    volume = volume.reshape(SLAB, CELLS, CIN)
    cot = cotangent.reshape(SLAB * CELLS, COUT)
    weight = weight.reshape(TAPS * CIN, COUT)

    before, after = neighbours(volume[SLAB - 1], 1), neighbours(volume[0], -1)
    inner, turned, share = local_share(row_order(), volume, cot)
    before, after, inner, turned, share = together(before, after, inner, turned, share)
    outer, keep, send = edge_share(before, after, turned, share)

    received = swapped(send, 0)
    weight, send = together(weight, send)
    back_weight = turn_weight(weight)
    received, back_weight = together(received, back_weight)
    keep, send = halved(keep, received, 0)

    received = swapped(send, 1)
    weight, send = together(weight, send)
    activation = forward(0, inner, outer, weight, None)
    cot, activation = together(cot, activation)
    cot_before = neighbours(cot[(SLAB - 1) * CELLS :], 1)
    cot_after = neighbours(cot[:CELLS], -1)
    received, activation = together(received, activation)
    keep, send = halved(keep, received, 1)

    received = swapped(send, 2)
    weight, send = together(weight, send)
    activation = forward(1, inner, outer, weight, activation)
    received, activation, cot_before, cot_after = together(received, activation, cot_before, cot_after)
    keep, send = halved(keep, received, 2)

    received = swapped(send, 3)
    back_weight, send = together(back_weight, send)
    input_grad = input_grad_plane(0, cot_before, cot, cot_after, back_weight, None)
    received, input_grad = together(received, input_grad)
    keep, send = halved(keep, received, 3)

    received = swapped(send, 4)
    back_weight, send = together(back_weight, send)
    input_grad = input_grad_plane(1, cot_before, cot, cot_after, back_weight, input_grad)
    received, input_grad = together(received, input_grad)

    for stage in range(4, 7):
        keep, send = halved(keep, received, stage)
        received = swapped(send, stage + 1)
    total = keep + received
    count = lax.axis_size("dp") * lax.axis_size("space") * SLAB * CELLS
    return (
        activation.reshape(1, SLAB, SIDE, SIDE, COUT),
        input_grad.reshape(1, SLAB, SIDE, SIDE, CIN),
        total / jnp.sqrt(f32(count)),
    )


def solution(mesh):
    slabs = P("dp", "space", None, None, None)
    return jax.shard_map(
        shards,
        mesh=mesh,
        in_specs=(slabs, P(), slabs),
        out_specs=(slabs, slabs, P(("dp", "space"), None)),
        check_vma=False,
    )
```

time: 80.3 us -> 66.3 us (0.83)
  waiting for transfers between devices: 19.8 us -> 10.6 us
  starting transfers between devices: 37.3 us -> 32.2 us
  local copies, waits for them, and re-layouts: 1.76 us -> 3.55 us
  Pallas kernels: 19.3 us -> 17.8 us
    pallas_call x3, Pallas kernels: 19.3 us -> 5.45 us  [call(): pl.pallas_call(kernel, out_shape=outs, in_specs=[in_vmem()] * len(args),...]
    pallas_call x0 -> x4, Pallas kernels: none -> 12.3 us  [call_for_plane(): pl.pallas_call(kernel, out_shape=jax.ShapeDtypeStruct((SLAB * CELLS, lane...]
    ppermute x8, waiting for transfers between devices: 16.1 us -> 10.6 us  [swapped(): return lax.ppermute(send, ('dp', 'space'), partners(stage))]
    ppermute x4, starting transfers between devices: 11.7 us -> 7.75 us  [neighbours(): return lax.ppermute(value, 'space', pairs)]
    ppermute x4, waiting for transfers between devices: 3.76 us -> 0.01 us  [neighbours(): return lax.ppermute(value, 'space', pairs)]
    unnamed x6, local copies, waits for them, and re-layouts: 0.36 us -> 2.27 us
    ppermute x8, starting transfers between devices: 25.6 us -> 24.5 us  [swapped(): return lax.ppermute(send, ('dp', 'space'), partners(stage))]
  transfers between devices with their start and end apart: 12 -> 12, of which waited for: 8 -> 6; matrix products, arithmetic and copies ran while one was open for 0% -> 0% of each run, Pallas kernels for 24% -> 24%
where the time goes in v2:
time: 66.3 us; the launch traced here: 66 us
  starting transfers between devices  32.2 us (49%)
  Pallas kernels  17.8 us (27%)
  waiting for transfers between devices  10.6 us (16%)
  local copies, waits for them, and re-layouts  3.55 us (5%)
  other arithmetic  1.09 us (2%)
  between operations  0.86 us (1%)
    ppermute x8, starting transfers between devices, swapped(): return lax.ppermute(send, ('dp', 'space'), partners(stage))  24.5 us
    pallas_call x4, Pallas kernels, call_for_plane(): pl.pallas_call(kernel, out_shape=jax.ShapeDtypeStruct((SLAB * CELLS, lane...  12.3 us
    ppermute x8, waiting for transfers between devices, swapped(): return lax.ppermute(send, ('dp', 'space'), partners(stage))  10.6 us
    ppermute x4, starting transfers between devices, neighbours(): return lax.ppermute(value, 'space', pairs)  7.75 us
    pallas_call x3, Pallas kernels, call(): pl.pallas_call(kernel, out_shape=outs, in_specs=[in_vmem()] * len(args),...  5.45 us
    unnamed x6, local copies, waits for them, and re-layouts  2.27 us
  transfers between devices with their start and end apart: 12, of which 6 were waited for; matrix products, arithmetic and copies ran while one was open for 0% of the time, Pallas kernels for 24%

profile of v2, /device:TPU:6, one launch (start us, length us, event | category | flops | bytes accessed | tf_op | source)
XLA Modules:
  0.0 66.0 jit_solution(8337255549105016643)
XLA Ops:
  0.6 1.1 %fusion.26 = (bf16[1,1,32,32,128]{4,3,2,1,0:T(8,128)(2,1)S(1)}, bf16[1,1,32,32,128]{4,3,2,1,0:T(8,128)(2,1)S(1)}) fusion(bf16[1,2,32,32,128]{4,3,2,1,0:T(8,128)(2,1)} %param.3), kind=kLoop, calls=%fused_computation.51 | loop fusion | bytes 1048576 | tf_op jit(solution)/shard_map/slice | solution.py:267
  1.7 1.8 %collective-permute-start = (bf16[1024,128]{1,0:T(8,128)(2,1)S(1)}, bf16[1024,128]{1,0:T(8,128)(2,1)S(1)}, u32[]{:S(2)}, u32[]{:S(2)}) collective-permute-start(bf16[1024,128]{1,0:T(8,128)(2,1)S(1)} %bitcast.17), channel_id=1, source_target_pairs={{0,1},{1,2},{2,3},{3,4},{4,5},{5,6},{6,7},{7,8},{8,9},{9,10},{10,1... | collective-permute-start | bytes 786440 | tf_op jit(solution)/shard_map/ppermute | solution.py:210
  3.5 1.3 %collective-permute-start.1 = (bf16[1024,128]{1,0:T(8,128)(2,1)S(1)}, bf16[1024,128]{1,0:T(8,128)(2,1)S(1)}, u32[]{:S(2)}, u32[]{:S(2)}) collective-permute-start(bf16[1024,128]{1,0:T(8,128)(2,1)S(1)} %bitcast.16), channel_id=1, source_target_pairs={{1,0},{2,1},{3,2},{4,3},{5,4},{6,5},{7,6},{8,7},{9,8},{10,9},{11,1... | collective-permute-start | bytes 786440 | tf_op jit(solution)/shard_map/ppermute | solution.py:210
  4.8 0.1 fusion.order
  5.0 1.2 %copy-done.1 = bf16[1,2,32,32,256]{4,3,2,1,0:T(8,128)(2,1)S(1)} copy-done((bf16[1,2,32,32,256]{4,3,2,1,0:T(8,128)(2,1)S(1)}, bf16[1,2,32,32,256]{4,3,2,1,0:T(8,128)(2,1)}, u32[]{:S(2)}) %copy-start.1) | copy-done | bytes 1048600
  6.2 1.0 %copy-done.2 = bf16[1,2,32,32,128]{4,3,2,1,0:T(8,128)(2,1)S(1)} copy-done((bf16[1,2,32,32,128]{4,3,2,1,0:T(8,128)(2,1)S(1)}, bf16[1,2,32,32,128]{4,3,2,1,0:T(8,128)(2,1)}, u32[]{:S(2)}) %copy-start.2) | copy-done | bytes 524312
  7.2 3.3 %local_share.1 = (bf16[2,1088,384]{2,1,0:T(8,128)(2,1)S(1)}, bf16[256,2048]{1,0:T(8,128)(2,1)S(1)}, f32[256,3456]{1,0:T(8,128)S(1)}) custom-call(bf16[256,256]{1,0:T(8,128)(2,1)S(1)} %fusion.order, bf16[2,1024,128]{2,1,0:T(8,128)(2,1)S(1)} %bitcast.14, bf16[2048,256]{1,0:T(8,128)(2,1)S(1)} %bitcast.10), custom_call_target="tpu_custom_call" | custom-call | flops 2415919104 | bytes 4194304 | tf_op jit(solution)/shard_map/local_share/pallas_call | solution.py:24
  10.5 1.7 %edge_share.1 = (bf16[2,1088,384]{2,1,0:T(8,128)(2,1)S(1)}, f32[128,3456]{1,0:T(8,128)S(1)}, bf16[128,3456]{1,0:T(8,128)(2,1)S(1)}) custom-call(bf16[1024,128]{1,0:T(8,128)(2,1)S(1)} %collective-permute-done.before, bf16[1024,128]{1,0:T(8,128)(2,1)S(1)} %collective-permute-done.1.after, bf16[256,2048]{1,0:T(8,128)(2,1)S(1)} %get-tuple-element.38.turned, ...), custom_call_target="tpu_custom_call" | custom-call | flops 1207959552 | bytes 4194304 | tf_op jit(solution)/shard_map/edge_share/pallas_call | solution.py:24
  12.2 2.9 %collective-permute-start.2 = (bf16[128,3456]{1,0:T(8,128)(2,1)S(1)}, bf16[128,3456]{1,0:T(8,128)(2,1)S(1)}, u32[]{:S(2)}, u32[]{:S(2)}) collective-permute-start(bf16[128,3456]{1,0:T(8,128)(2,1)S(1)} %get-tuple-element.41), channel_id=1, source_target_pairs={{0,1},{1,0},{2,3},{3,2},{4,5},{5,4},{6,7},{7,6},{8,9},{9,8},{10,11... | collective-permute-start | bytes 2654216 | tf_op jit(solution)/shard_map/ppermute | solution.py:253
  15.1 0.5 turn_weight.1.turned
  15.6 1.5 %collective-permute-done.2 = bf16[128,3456]{1,0:T(8,128)(2,1)S(1)} collective-permute-done((bf16[128,3456]{1,0:T(8,128)(2,1)S(1)}, bf16[128,3456]{1,0:T(8,128)(2,1)S(1)}, u32[]{:S(2)}, u32[]{:S(2)}) %collective-permute-start.2) | collective-permute-done | bytes 884768 | tf_op jit(solution)/shard_map/ppermute | solution.py:253
  17.2 0.1 convert_add_fusion
  17.4 0.9 %collective-permute-start.3 = (bf16[64,3456]{1,0:T(8,128)(2,1)S(1)}, bf16[64,3456]{1,0:T(8,128)(2,1)S(1)}, u32[]{:S(2)}, u32[]{:S(2)}) collective-permute-start(bf16[64,3456]{1,0:T(8,128)(2,1)S(1)} %slice.107), channel_id=1, source_target_pairs={{0,64},{1,17},{2,66},{3,19},{4,68},{5,21},{6,70},{7,23},{8,72},{9,... | collective-permute-start | bytes 1327112 | tf_op jit(solution)/shard_map/ppermute | solution.py:253
  18.3 2.9 %forward_0.1.rest_0_ = bf16[2048,256]{1,0:T(8,128)(2,1)} custom-call(bf16[2,1088,384]{2,1,0:T(8,128)(2,1)S(1)} %get-tuple-element.44.inner, bf16[2,1088,384]{2,1,0:T(8,128)(2,1)S(1)} %get-tuple-element.45.outer, bf16[3456,256]{1,0:T(8,128)(2,1)S(1)} %bitcast.8), custom_call_target="tpu_custom_call" | custom-call | flops 1811939328 | bytes 4194304 | tf_op jit(solution)/shard_map/forward_0/pallas_call | solution.py:42
  21.2 1.3 %collective-permute-start.6 = (bf16[1024,256]{1,0:T(8,128)(2,1)S(1)}, bf16[1024,256]{1,0:T(8,128)(2,1)S(1)}, u32[]{:S(2)}, u32[]{:S(2)}) collective-permute-start(bf16[1024,256]{1,0:T(8,128)(2,1)S(1)} %get-tuple-element.63), channel_id=1, source_target_pairs={{1,0},{2,1},{3,2},{4,3},{5,4},{6,5},{7,6},{8,7},{9,8},{10,9},{11,1... | collective-permute-start | bytes 1572872 | tf_op jit(solution)/shard_map/ppermute | solution.py:210
  22.5 3.4 %collective-permute-start.5 = (bf16[1024,256]{1,0:T(8,128)(2,1)S(1)}, bf16[1024,256]{1,0:T(8,128)(2,1)S(1)}, u32[]{:S(2)}, u32[]{:S(2)}) collective-permute-start(bf16[1024,256]{1,0:T(8,128)(2,1)S(1)} %get-tuple-element.64), channel_id=1, source_target_pairs={{0,1},{1,2},{2,3},{3,4},{4,5},{5,6},{6,7},{7,8},{8,9},{9,10},{10,1... | collective-permute-start | bytes 1572872 | tf_op jit(solution)/shard_map/ppermute | solution.py:210
  25.9 0.1 slice_add_fusion
  26.1 1.5 %collective-permute-start.4 = (bf16[32,3456]{1,0:T(8,128)(2,1)S(1)}, bf16[32,3456]{1,0:T(8,128)(2,1)S(1)}, u32[]{:S(2)}, u32[]{:S(2)}) collective-permute-start(bf16[32,3456]{1,0:T(8,128)(2,1)S(1)} %slice.108), channel_id=1, source_target_pairs={{0,16},{1,65},{2,18},{3,67},{4,20},{5,69},{6,22},{7,71},{8,24},{9,... | collective-permute-start | bytes 663560 | tf_op jit(solution)/shard_map/ppermute | solution.py:253
  27.5 2.9 %forward_1.1 = bf16[2048,256]{1,0:T(8,128)(2,1)} custom-call(bf16[2,1088,384]{2,1,0:T(8,128)(2,1)S(1)} %get-tuple-element.44.inner, bf16[2,1088,384]{2,1,0:T(8,128)(2,1)S(1)} %get-tuple-element.45.outer, bf16[3456,256]{1,0:T(8,128)(2,1)S(1)} %bitcast.9, bf16[2048,256]{1,0:T(8,128)(2,1)} %forward_0.1.rest_0_), custom_call_target="tpu_custom_call", output_to_operand_aliasing={{}: (3, {})} | custom-call | flops 1811939328 | bytes 4194304 | tf_op jit(solution)/shard_map/forward_1/pallas_call | solution.py:42
  30.4 1.7 %collective-permute-done.4 = bf16[32,3456]{1,0:T(8,128)(2,1)S(1)} collective-permute-done((bf16[32,3456]{1,0:T(8,128)(2,1)S(1)}, bf16[32,3456]{1,0:T(8,128)(2,1)S(1)}, u32[]{:S(2)}, u32[]{:S(2)}) %collective-permute-start.4) | collective-permute-done | bytes 221216 | tf_op jit(solution)/shard_map/ppermute | solution.py:253
  32.1 0.9 %collective-permute-start.7 = (bf16[16,3456]{1,0:T(8,128)(2,1)S(1)}, bf16[16,3456]{1,0:T(8,128)(2,1)S(1)}, u32[]{:S(2)}, u32[]{:S(2)}) collective-permute-start(bf16[16,3456]{1,0:T(8,128)(2,1)S(1)} %slice.109), channel_id=1, source_target_pairs={{0,192},{1,49},{2,194},{3,51},{4,196},{5,53},{6,198},{7,55},{8,200... | collective-permute-start | bytes 331784 | tf_op jit(solution)/shard_map/ppermute | solution.py:253
  33.0 3.3 %input_grad_0.1.rest_0_ = bf16[2048,128]{1,0:T(8,128)(2,1)} custom-call(bf16[1024,256]{1,0:T(8,128)(2,1)S(1)} %collective-permute-done.5.before, bf16[2048,256]{1,0:T(8,128)(2,1)S(1)} %bitcast.12, bf16[1024,256]{1,0:T(8,128)(2,1)S(1)} %collective-permute-done.6.after, bf16[2304,384]{1,0:T(8,128)(2,1)S(1)} %turn_weight.1.turned), custom_call_target="tpu_custom_call" | custom-call | flops 1811939328 | bytes 4194304 | tf_op jit(solution)/shard_map/input_grad_0/pallas_call | solution.py:42
  36.3 1.9 %collective-permute-done.7 = bf16[16,3456]{1,0:T(8,128)(2,1)S(1)} collective-permute-done((bf16[16,3456]{1,0:T(8,128)(2,1)S(1)}, bf16[16,3456]{1,0:T(8,128)(2,1)S(1)}, u32[]{:S(2)}, u32[]{:S(2)}) %collective-permute-start.7) | collective-permute-done | bytes 110624 | tf_op jit(solution)/shard_map/ppermute | solution.py:253
  38.2 3.1 %collective-permute-start.8 = (bf16[8,3456]{1,0:T(8,128)(2,1)S(1)}, bf16[8,3456]{1,0:T(8,128)(2,1)S(1)}, u32[]{:S(2)}, u32[]{:S(2)}) collective-permute-start(bf16[8,3456]{1,0:T(8,128)(2,1)S(1)} %slice.110), channel_id=1, source_target_pairs={{0,48},{1,193},{2,50},{3,195},{4,52},{5,197},{6,54},{7,199},{8,56}... | collective-permute-start | bytes 165896 | tf_op jit(solution)/shard_map/ppermute | solution.py:253
  41.3 3.3 %input_grad_1.1 = bf16[2048,128]{1,0:T(8,128)(2,1)} custom-call(bf16[1024,256]{1,0:T(8,128)(2,1)S(1)} %collective-permute-done.5.before, bf16[2048,256]{1,0:T(8,128)(2,1)S(1)} %bitcast.13, bf16[1024,256]{1,0:T(8,128)(2,1)S(1)} %collective-permute-done.6.after, bf16[2304,384]{1,0:T(8,128)(2,1)S(1)} %turn_weight.1.turned, ...), custom_call_target="tpu_custom_call", output_to_operand_aliasing={{}: (4, {})} | custom-call | flops 1811939328 | bytes 4194304 | tf_op jit(solution)/shard_map/input_grad_1/pallas_call | solution.py:42
  44.7 3.8 %collective-permute-start.9 = (bf16[4,3456]{1,0:T(4,128)(2,1)S(1)}, bf16[4,3456]{1,0:T(4,128)(2,1)S(1)}, u32[]{:S(2)}, u32[]{:S(2)}) collective-permute-start(bf16[4,3456]{1,0:T(4,128)(2,1)S(1)} %slice.111), channel_id=1, source_target_pairs={{0,2},{1,3},{2,0},{3,1},{4,6},{5,7},{6,4},{7,5},{8,10},{9,11},{10,... | collective-permute-start | bytes 82952 | tf_op jit(solution)/shard_map/ppermute | solution.py:253
  48.5 1.8 %collective-permute-done.9 = bf16[4,3456]{1,0:T(4,128)(2,1)S(1)} collective-permute-done((bf16[4,3456]{1,0:T(4,128)(2,1)S(1)}, bf16[4,3456]{1,0:T(4,128)(2,1)S(1)}, u32[]{:S(2)}, u32[]{:S(2)}) %collective-permute-start.9) | collective-permute-done | bytes 27680 | tf_op jit(solution)/shard_map/ppermute | solution.py:253
  50.4 7.0 %collective-permute-start.10 = (f32[2,3456]{1,0:T(2,128)S(1)}, f32[2,3456]{1,0:T(2,128)S(1)}, u32[]{:S(2)}, u32[]{:S(2)}) collective-permute-start(f32[2,3456]{1,0:T(2,128)S(1)} %slice.90), channel_id=1, source_target_pairs={{0,14},{1,15},{2,4},{3,5},{4,2},{5,3},{6,8},{7,9},{8,6},{9,7},{10,... | collective-permute-start | bytes 82952 | tf_op jit(solution)/shard_map/ppermute | solution.py:253
  57.4 1.8 %collective-permute-done.10 = f32[2,3456]{1,0:T(2,128)S(1)} collective-permute-done((f32[2,3456]{1,0:T(2,128)S(1)}, f32[2,3456]{1,0:T(2,128)S(1)}, u32[]{:S(2)}, u32[]{:S(2)}) %collective-permute-start.10) | collective-permute-done | bytes 27680 | tf_op jit(solution)/shard_map/ppermute | solution.py:253
  59.3 4.3 %collective-permute-start.11 = (f32[1,3456]{1,0:T(1,128)S(1)}, f32[1,3456]{1,0:T(1,128)S(1)}, u32[]{:S(2)}, u32[]{:S(2)}) collective-permute-start(f32[1,3456]{1,0:T(1,128)S(1)} %slice.92), channel_id=1, source_target_pairs={{0,6},{1,7},{2,12},{3,13},{4,10},{5,11},{6,0},{7,1},{8,14},{9,15},... | collective-permute-start | bytes 41480 | tf_op jit(solution)/shard_map/ppermute | solution.py:253
  63.6 1.8 %collective-permute-done.11 = f32[1,3456]{1,0:T(1,128)S(1)} collective-permute-done((f32[1,3456]{1,0:T(1,128)S(1)}, f32[1,3456]{1,0:T(1,128)S(1)}, u32[]{:S(2)}, u32[]{:S(2)}) %collective-permute-start.11) | collective-permute-done | bytes 13856 | tf_op jit(solution)/shard_map/ppermute | solution.py:253
  65.4 0.6 fusion.1
  (24 shorter events, 0.4 us)
Async XLA Ops:
  1.7 8.8 %collective-permute-start = (bf16[1024,128]{1,0:T(8,128)(2,1)S(1)}, bf16[1024,128]{1,0:T(8,128)(2,1)S(1)}, u32[]{:S(2)}, u32[]{:S(2)}) collective-permute-start(bf16[1024,128]{1,0:T(8,128)(2,1)S(1)} %bitcast.17), channel_id=1, source_target_pairs={{0,1},{1,2},{2,3},{3,4},{4,5},{5,6},{6,7},{7,8},{8,9},{9,10},{10,1... | collective-permute-start | bytes 786440 | tf_op jit(solution)/shard_map/ppermute | solution.py:210
  3.5 7.0 %collective-permute-start.1 = (bf16[1024,128]{1,0:T(8,128)(2,1)S(1)}, bf16[1024,128]{1,0:T(8,128)(2,1)S(1)}, u32[]{:S(2)}, u32[]{:S(2)}) collective-permute-start(bf16[1024,128]{1,0:T(8,128)(2,1)S(1)} %bitcast.16), channel_id=1, source_target_pairs={{1,0},{2,1},{3,2},{4,3},{5,4},{6,5},{7,6},{8,7},{9,8},{10,9},{11,1... | collective-permute-start | bytes 786440 | tf_op jit(solution)/shard_map/ppermute | solution.py:210
  5.0 1.2 %copy-start.1 = (bf16[1,2,32,32,256]{4,3,2,1,0:T(8,128)(2,1)S(1)}, bf16[1,2,32,32,256]{4,3,2,1,0:T(8,128)(2,1)}, u32[]{:S(2)}) copy-start(bf16[1,2,32,32,256]{4,3,2,1,0:T(8,128)(2,1)} %param.5) | copy-start | bytes 3145732
  6.2 1.0 %copy-start.2 = (bf16[1,2,32,32,128]{4,3,2,1,0:T(8,128)(2,1)S(1)}, bf16[1,2,32,32,128]{4,3,2,1,0:T(8,128)(2,1)}, u32[]{:S(2)}) copy-start(bf16[1,2,32,32,128]{4,3,2,1,0:T(8,128)(2,1)} %param.3) | copy-start | bytes 1572868
  10.5 4.6 %copy-start = (bf16[27,128,256]{2,1,0:T(8,128)(2,1)S(1)}, bf16[27,128,256]{2,1,0:T(8,128)(2,1)}, u32[]{:S(2)}) copy-start(bf16[27,128,256]{2,1,0:T(8,128)(2,1)} %param.4) | copy-start | bytes 5308420
  12.2 5.0 %collective-permute-start.2 = (bf16[128,3456]{1,0:T(8,128)(2,1)S(1)}, bf16[128,3456]{1,0:T(8,128)(2,1)S(1)}, u32[]{:S(2)}, u32[]{:S(2)}) collective-permute-start(bf16[128,3456]{1,0:T(8,128)(2,1)S(1)} %get-tuple-element.41), channel_id=1, source_target_pairs={{0,1},{1,0},{2,3},{3,2},{4,5},{5,4},{6,7},{7,6},{8,9},{9,8},{10,11... | collective-permute-start | bytes 2654216 | tf_op jit(solution)/shard_map/ppermute | solution.py:253
  17.4 8.6 %collective-permute-start.3 = (bf16[64,3456]{1,0:T(8,128)(2,1)S(1)}, bf16[64,3456]{1,0:T(8,128)(2,1)S(1)}, u32[]{:S(2)}, u32[]{:S(2)}) collective-permute-start(bf16[64,3456]{1,0:T(8,128)(2,1)S(1)} %slice.107), channel_id=1, source_target_pairs={{0,64},{1,17},{2,66},{3,19},{4,68},{5,21},{6,70},{7,23},{8,72},{9,... | collective-permute-start | bytes 1327112 | tf_op jit(solution)/shard_map/ppermute | solution.py:253
  21.2 9.2 %collective-permute-start.6 = (bf16[1024,256]{1,0:T(8,128)(2,1)S(1)}, bf16[1024,256]{1,0:T(8,128)(2,1)S(1)}, u32[]{:S(2)}, u32[]{:S(2)}) collective-permute-start(bf16[1024,256]{1,0:T(8,128)(2,1)S(1)} %get-tuple-element.63), channel_id=1, source_target_pairs={{1,0},{2,1},{3,2},{4,3},{5,4},{6,5},{7,6},{8,7},{9,8},{10,9},{11,1... | collective-permute-start | bytes 1572872 | tf_op jit(solution)/shard_map/ppermute | solution.py:210
  22.5 7.9 %collective-permute-start.5 = (bf16[1024,256]{1,0:T(8,128)(2,1)S(1)}, bf16[1024,256]{1,0:T(8,128)(2,1)S(1)}, u32[]{:S(2)}, u32[]{:S(2)}) collective-permute-start(bf16[1024,256]{1,0:T(8,128)(2,1)S(1)} %get-tuple-element.64), channel_id=1, source_target_pairs={{0,1},{1,2},{2,3},{3,4},{4,5},{5,6},{6,7},{7,8},{8,9},{9,10},{10,1... | collective-permute-start | bytes 1572872 | tf_op jit(solution)/shard_map/ppermute | solution.py:210
  26.1 6.0 %collective-permute-start.4 = (bf16[32,3456]{1,0:T(8,128)(2,1)S(1)}, bf16[32,3456]{1,0:T(8,128)(2,1)S(1)}, u32[]{:S(2)}, u32[]{:S(2)}) collective-permute-start(bf16[32,3456]{1,0:T(8,128)(2,1)S(1)} %slice.108), channel_id=1, source_target_pairs={{0,16},{1,65},{2,18},{3,67},{4,20},{5,69},{6,22},{7,71},{8,24},{9,... | collective-permute-start | bytes 663560 | tf_op jit(solution)/shard_map/ppermute | solution.py:253
  32.1 6.0 %collective-permute-start.7 = (bf16[16,3456]{1,0:T(8,128)(2,1)S(1)}, bf16[16,3456]{1,0:T(8,128)(2,1)S(1)}, u32[]{:S(2)}, u32[]{:S(2)}) collective-permute-start(bf16[16,3456]{1,0:T(8,128)(2,1)S(1)} %slice.109), channel_id=1, source_target_pairs={{0,192},{1,49},{2,194},{3,51},{4,196},{5,53},{6,198},{7,55},{8,200... | collective-permute-start | bytes 331784 | tf_op jit(solution)/shard_map/ppermute | solution.py:253
  38.2 6.4 %collective-permute-start.8 = (bf16[8,3456]{1,0:T(8,128)(2,1)S(1)}, bf16[8,3456]{1,0:T(8,128)(2,1)S(1)}, u32[]{:S(2)}, u32[]{:S(2)}) collective-permute-start(bf16[8,3456]{1,0:T(8,128)(2,1)S(1)} %slice.110), channel_id=1, source_target_pairs={{0,48},{1,193},{2,50},{3,195},{4,52},{5,197},{6,54},{7,199},{8,56}... | collective-permute-start | bytes 165896 | tf_op jit(solution)/shard_map/ppermute | solution.py:253
  44.7 5.7 %collective-permute-start.9 = (bf16[4,3456]{1,0:T(4,128)(2,1)S(1)}, bf16[4,3456]{1,0:T(4,128)(2,1)S(1)}, u32[]{:S(2)}, u32[]{:S(2)}) collective-permute-start(bf16[4,3456]{1,0:T(4,128)(2,1)S(1)} %slice.111), channel_id=1, source_target_pairs={{0,2},{1,3},{2,0},{3,1},{4,6},{5,7},{6,4},{7,5},{8,10},{9,11},{10,... | collective-permute-start | bytes 82952 | tf_op jit(solution)/shard_map/ppermute | solution.py:253
  50.4 8.8 %collective-permute-start.10 = (f32[2,3456]{1,0:T(2,128)S(1)}, f32[2,3456]{1,0:T(2,128)S(1)}, u32[]{:S(2)}, u32[]{:S(2)}) collective-permute-start(f32[2,3456]{1,0:T(2,128)S(1)} %slice.90), channel_id=1, source_target_pairs={{0,14},{1,15},{2,4},{3,5},{4,2},{5,3},{6,8},{7,9},{8,6},{9,7},{10,... | collective-permute-start | bytes 82952 | tf_op jit(solution)/shard_map/ppermute | solution.py:253
  59.3 6.1 %collective-permute-start.11 = (f32[1,3456]{1,0:T(1,128)S(1)}, f32[1,3456]{1,0:T(1,128)S(1)}, u32[]{:S(2)}, u32[]{:S(2)}) collective-permute-start(f32[1,3456]{1,0:T(1,128)S(1)} %slice.92), channel_id=1, source_target_pairs={{0,6},{1,7},{2,12},{3,13},{4,10},{5,11},{6,0},{7,1},{8,14},{9,15},... | collective-permute-start | bytes 41480 | tf_op jit(solution)/shard_map/ppermute | solution.py:253

commit v3 on v0

v3 whole, which is shorter than its diff:
```python
import jax
import jax.numpy as jnp
from jax import lax
from jax.experimental import pallas as pl
from jax.experimental.pallas import tpu as pltpu
from jax.sharding import PartitionSpec as P

bf16, f32 = jnp.bfloat16, jnp.float32
SIDE = 32
CELLS = SIDE * SIDE
CIN, COUT, TAPS = 128, 256, 27
SLAB = 2
PADDED = CELLS + 2 * SIDE
COLUMNS = TAPS * CIN
VMEM_SOME, VMEM_MOST = 24 << 20, 58 << 20
FLOPS = 2 * SLAB * CELLS * TAPS * CIN * COUT

IN_VMEM = pl.BlockSpec(memory_space=pltpu.VMEM)
IN_SMEM = pl.BlockSpec(memory_space=pltpu.SMEM)
IN_HBM = pl.BlockSpec(memory_space=pltpu.HBM)


def shaped(kind, *shape):
    return jax.ShapeDtypeStruct(shape, kind)


def call(kernel, outs, args, scratch=(), flops=1 << 20, specs=None, vmem=VMEM_SOME, **options):
    if specs is None:
        specs = [IN_VMEM if a.ndim > 1 else IN_SMEM for a in args]
    options.setdefault("out_specs", tuple(IN_VMEM for _ in outs))
    return pl.pallas_call(
        kernel,
        out_shape=outs,
        in_specs=specs,
        scratch_shapes=list(scratch),
        compiler_params=pltpu.CompilerParams(vmem_limit_bytes=vmem),
        cost_estimate=pl.CostEstimate(flops=flops, bytes_accessed=4 << 20, transcendentals=0),
        **options,
    )(*args)


def product(a, b):
    return jnp.dot(a, b, preferred_element_type=f32)


def fill_taps(plane, i, wide, taps):
    col = lax.broadcasted_iota(jnp.int32, (CELLS, CIN), 0) % SIDE
    zero = jnp.zeros((SIDE, 3 * CIN), bf16)
    inner = pl.ds(SIDE, CELLS)
    wide[pl.ds(8, CELLS), :] = plane[...].astype(f32)
    taps[i, pl.ds(0, SIDE), :] = zero
    taps[i, pl.ds(SIDE + CELLS, SIDE), :] = zero
    left = jnp.where(col > 0, wide[pl.ds(7, CELLS), :], 0.0)
    right = jnp.where(col < SIDE - 1, wide[pl.ds(9, CELLS), :], 0.0)
    taps[i, inner, pl.ds(0, CIN)] = left.astype(bf16)
    taps[i, inner, pl.ds(CIN, CIN)] = plane[...]
    taps[i, inner, pl.ds(2 * CIN, CIN)] = right.astype(bf16)


def taps_scratch(planes):
    return [pltpu.VMEM((CELLS + 16, CIN), f32), pltpu.VMEM((planes, PADDED, 3 * CIN), bf16)]


def taps_at(taps, plane, some):
    parts = [taps[plane, pl.ds(k // 3 % 3 * SIDE, CELLS), pl.ds(k % 3 * CIN, CIN)] for k in some]
    return jnp.concatenate(parts, axis=1)


def tap_groups(kd):
    return [range(k, min(k + 2, 9 * kd + 9)) for k in range(9 * kd, 9 * kd + 9, 2)]


def local_share_kernel(core, order, volume, cot, cot_near, cot_far, turned, share, wide, taps):
    c = core[0]
    cot_near[...] = cot[pl.ds(pl.multiple_of((1 - c) * CELLS, CELLS), CELLS), :]
    cot_far[...] = cot[pl.ds(pl.multiple_of(c * CELLS, CELLS), CELLS), :]
    for i in range(SLAB):
        fill_taps(volume.at[i], i, wide, taps)
    for j in range(SLAB * CELLS // 256):
        rows = pl.ds(j * 256, 256)
        turned[:, rows] = lax.dot_general(
            order[...], cot[rows, :], (((1,), (1,)), ((), ())), preferred_element_type=f32
        ).astype(bf16)
    for kd in range(3):
        for some in tap_groups(kd):
            total = None
            for d in range(SLAB):
                if 0 <= d + kd - 1 < SLAB:
                    part = product(turned[:, pl.ds(d * CELLS, CELLS)], taps_at(taps, d + kd - 1, some))
                    total = part if total is None else total + part
            share[:, pl.ds(some[0] * CIN, len(some) * CIN)] = total


def local_share(*args):
    plane = shaped(bf16, CELLS, COUT)
    outs = (plane, plane, shaped(bf16, COUT, SLAB * CELLS), shaped(f32, COUT, COLUMNS))
    return call(local_share_kernel, outs, args, taps_scratch(2), FLOPS * 2 // 3, name="local_share")


def edge_share_kernel(core, near, far, turned, share, keep, send, wide, taps):
    c = core[0]
    fill_taps(near, 1 - c, wide, taps)
    fill_taps(far, c, wide, taps)
    for kd in range(3):
        for some in tap_groups(kd):
            lanes = pl.ds(some[0] * CIN, len(some) * CIN)
            total = share[:, lanes]
            if kd != 1:
                edge = kd // 2
                total = total + product(turned[:, pl.ds(edge * CELLS, CELLS)], taps_at(taps, edge, some))
            keep[:, lanes] = total[: COUT // 2]
            send[:, lanes] = total[COUT // 2 :].astype(bf16)


def edge_share(core, near, far, turned, share):
    outs = (shaped(f32, COUT // 2, COLUMNS), shaped(bf16, COUT // 2, COLUMNS))
    args = (core, near, far, turned, share)
    return call(edge_share_kernel, outs, args, taps_scratch(2), FLOPS // 3, name="edge_share")


def forward_kernel(core, near, volume, far, weight, out, wide, taps):
    c = core[0]
    step = pl.program_id(0)

    @pl.when(step == 0)
    def _():
        for i in range(SLAB):
            fill_taps(volume.at[i], 1 + i, wide, taps)
        fill_taps(near, 3 * (1 - c), wide, taps)
        fill_taps(far, 3 * c, wide, taps)

    parts = []
    for k in range(TAPS):
        parts.append(taps[step + k // 9, pl.ds(k // 3 % 3 * SIDE, CELLS), pl.ds(k % 3 * CIN, CIN)])
    pre = product(jnp.concatenate(parts, axis=1), weight[...])
    out[...] = jnp.where(pre >= 0, pre, 0.3 * pre).astype(bf16)


def forward(*args):
    return call(
        forward_kernel,
        (shaped(bf16, SLAB * CELLS, COUT),),
        args,
        taps_scratch(4),
        FLOPS,
        grid=(SLAB,),
        out_specs=(pl.BlockSpec((CELLS, COUT), lambda i: (i, 0)),),
        vmem=VMEM_MOST,
        name="forward",
    )[0]


def turn_weight_kernel(weight, turned):
    for k in range(TAPS):
        turned[pl.ds(k // 3 * COUT, COUT), pl.ds(k % 3 * CIN, CIN)] = weight[pl.ds(k * CIN, CIN), :].T


def turn_weight(weight):
    return call(turn_weight_kernel, (shaped(bf16, 9 * COUT, 3 * CIN),), (weight,), name="turn_weight")[0]


def input_grad_kernel(core, near, cot, far, turned, out, padded, sums):
    c = core[0]
    step = pl.program_id(0)
    middle = pl.ds(SIDE, CELLS)

    @pl.when(step == 0)
    def _():
        zero = jnp.zeros((SIDE, COUT), bf16)
        for i in range(4):
            padded[i, pl.ds(0, SIDE), :] = zero
            padded[i, pl.ds(SIDE + CELLS, SIDE), :] = zero
        for i in range(SLAB):
            padded[1 + i, middle, :] = cot[pl.ds(i * CELLS, CELLS), :]
        padded[3 * (1 - c), middle, :] = near[...]
        padded[3 * c, middle, :] = far[...]

    parts = [padded[step + 2 - j // 3, pl.ds((2 - j % 3) * SIDE, CELLS), :] for j in range(9)]
    sums[pl.ds(8, CELLS), :] = product(jnp.concatenate(parts, axis=1), turned[...])
    col = lax.broadcasted_iota(jnp.int32, (CELLS, CIN), 0) % SIDE
    total = sums[pl.ds(8, CELLS), pl.ds(CIN, CIN)]
    total = total + jnp.where(col < SIDE - 1, sums[pl.ds(9, CELLS), pl.ds(0, CIN)], 0.0)
    total = total + jnp.where(col > 0, sums[pl.ds(7, CELLS), pl.ds(2 * CIN, CIN)], 0.0)
    out[...] = total.astype(bf16)


def input_grad_of(*args):
    return call(
        input_grad_kernel,
        (shaped(bf16, SLAB * CELLS, CIN),),
        args,
        [pltpu.VMEM((4, PADDED, COUT), bf16), pltpu.VMEM((CELLS + 16, 3 * CIN), f32)],
        FLOPS,
        grid=(SLAB,),
        out_specs=(pl.BlockSpec((CELLS, CIN), lambda i: (i, 0)),),
        vmem=VMEM_MOST,
        name="input_grad",
    )[0]


def from_core(value):
    return lax.ppermute(value, "space", [(i, i ^ 1) for i in range(16)])


def from_chip(value):
    return lax.ppermute(value, "space", [(i, ((i + 1) ^ 1) - 1) for i in range(1, 15)])


def row_order(core):
    place = lax.iota(jnp.int32, COUT)
    row = (place & 127) * 2 + (core ^ (place >> 7))
    return (row[:, None] == lax.iota(jnp.int32, COUT)[None, :]).astype(bf16)


def together(*arrays):
    return lax.optimization_barrier(arrays)


def shards(volume, weight, cotangent):
    volume = volume.reshape(SLAB, CELLS, CIN)
    cot = cotangent.reshape(SLAB * CELLS, COUT)
    weight = weight.reshape(COLUMNS, COUT)
    core = lax.axis_index("space").astype(jnp.int32) % 2
    flag = core.reshape(1)

    def plane(i):
        return lax.dynamic_index_in_dim(volume, i, 0, False)

    far, near = from_chip(plane(core)), from_core(plane(1 - core))
    cot_near, cot_far, turned, share = local_share(flag, row_order(core), volume, cot)
    far, near, turned, share = together(far, near, turned, share)
    keep, send = edge_share(flag, near, far, turned, share)

    received = from_core(send)
    weight, send = together(weight, send)
    back_weight = turn_weight(weight)
    cot_far, cot_near, back_weight = together(cot_far, cot_near, back_weight)
    cot_far, cot_near = from_chip(cot_far), from_core(cot_near)
    received, back_weight = together(received, back_weight)
    total = keep + received.astype(f32)

    dp = lax.axis_size("dp")
    send = total.astype(bf16).reshape(dp, -1, COLUMNS)
    parts = lax.all_to_all(send, "dp", 0, 0)
    weight, send = together(weight, send)
    activation = forward(flag, near, volume, far, weight)
    parts, activation = together(parts, activation)
    send = jnp.sum(parts.astype(f32), axis=0).reshape(8, 1, COLUMNS)

    parts = lax.all_to_all(send, "space", 0, 0, axis_index_groups=[list(range(c, 16, 2)) for c in range(2)])
    back_weight, send = together(back_weight, send)
    input_grad = input_grad_of(flag, cot_near, cot, cot_far, back_weight)
    parts, input_grad = together(parts, input_grad)
    count = dp * lax.axis_size("space") * SLAB * CELLS
    return (
        activation.reshape(1, SLAB, SIDE, SIDE, COUT),
        input_grad.reshape(1, SLAB, SIDE, SIDE, CIN),
        jnp.sum(parts, axis=0) / jnp.sqrt(f32(count)),
    )


def solution(mesh):
    slabs = P("dp", "space", None, None, None)
    return jax.shard_map(
        shards,
        mesh=mesh,
        in_specs=(slabs, P(), slabs),
        out_specs=(slabs, slabs, P(("dp", "space"), None)),
        check_vma=False,
    )
```

time: 363 us -> 59.8 us (0.16)
  the two profiles are of different devices: /device:TPU:6 before, /device:TPU:32 now
where the time goes in v3:
time: 59.8 us; the launch traced here: 59.4 us
  Pallas kernels  21.5 us (36%)
  starting transfers between devices  20.9 us (35%)
  local copies, waits for them, and re-layouts  7.5 us (13%)
  waiting for transfers between devices  7.24 us (12%)
  other arithmetic  1.42 us (2%)
  between operations  0.82 us (1%)
    pallas_call x5, Pallas kernels, call(): pl.pallas_call(kernel, out_shape=outs, in_specs=specs, scratch_shapes=lis...  21.5 us
    all_to_all x1, starting transfers between devices, shards(): lax.all_to_all(send, 'space', 0, 0, axis_index_groups=[list(range(c, 16,...  7.84 us
    all_to_all x1, starting transfers between devices, shards(): parts = lax.all_to_all(send, 'dp', 0, 0)  6.78 us
    all_to_all x1, waiting for transfers between devices, shards(): parts = lax.all_to_all(send, 'dp', 0, 0)  6.66 us
    ppermute x2, starting transfers between devices, from_chip(): lax.ppermute(value, 'space', [(i, (i + 1 ^ 1) - 1) for i in range(1, 15)])  5.88 us
    unnamed x16, local copies, waits for them, and re-layouts  5.1 us
  transfers between devices with their start and end apart: 7, of which 2 were waited for; matrix products, arithmetic and copies ran while one was open for 2% of the time, Pallas kernels for 33%

profile of v3, /device:TPU:32, one launch (start us, length us, event | category | flops | bytes accessed | tf_op | source)
XLA Modules:
  0.0 59.4 jit_solution(18205254872744967864)
XLA Ops:
  0.6 1.1 %dynamic-slice_bitcast_fusion = (bf16[1024,128]{1,0:T(8,128)(2,1)S(1)}, bf16[1024,128]{1,0:T(8,128)(2,1)S(1)}) fusion(bf16[2,1024,128]{2,1,0:T(8,128)(2,1)} %bitcast.14, s32[]{:T(128)S(6)} %select_n.16, s32[]{:T(128)S(6)} %select_n.15), kind=kLoop, calls=%fused_computation.4 | loop fusion | bytes 1048584 | tf_op jit(solution)/shard_map/jit(dynamic_index_in_dim)/squeeze | solution.py:227
  1.7 0.1 collective-permute-start.1
  1.8 3.8 %collective-permute-start = (bf16[1024,128]{1,0:T(8,128)(2,1)S(1)}, bf16[1024,128]{1,0:T(8,128)(2,1)S(1)}, u32[]{:S(2)}, u32[]{:S(2)}) collective-permute-start(bf16[1024,128]{1,0:T(8,128)(2,1)S(1)} %get-tuple-element.48), channel_id=1, source_target_pairs={{1,2},{2,1},{3,4},{4,3},{5,6},{6,5},{7,8},{8,7},{9,10},{10,9},{11,... | collective-permute-start | bytes 786440 | tf_op jit(solution)/shard_map/ppermute | solution.py:206
  5.7 0.1 fusion.1.order
  5.8 0.0 copy-start.2
  5.8 1.0 %copy-done.2 = bf16[1,2,32,32,128]{4,3,2,1,0:T(8,128)(2,1)S(1)} copy-done((bf16[1,2,32,32,128]{4,3,2,1,0:T(8,128)(2,1)S(1)}, bf16[1,2,32,32,128]{4,3,2,1,0:T(8,128)(2,1)}, u32[]{:S(2)}) %copy-start.2) | copy-done | bytes 524312
  6.8 1.2 %copy-done.5 = bf16[1,2,32,32,256]{4,3,2,1,0:T(8,128)(2,1)S(1)} copy-done((bf16[1,2,32,32,256]{4,3,2,1,0:T(8,128)(2,1)S(1)}, bf16[1,2,32,32,256]{4,3,2,1,0:T(8,128)(2,1)}, u32[]{:S(2)}) %copy-start.5) | copy-done | bytes 1048600
  8.1 3.4 %local_share.1 = (bf16[1024,256]{1,0:T(8,128)(2,1)S(1)}, bf16[1024,256]{1,0:T(8,128)(2,1)S(1)}, bf16[256,2048]{1,0:T(8,128)(2,1)S(1)}, f32[256,3456]{1,0:T(8,128)S(1)}) custom-call(s32[1]{0:T(128)} %bitcast.core, bf16[256,256]{1,0:T(8,128)(2,1)S(1)} %fusion.1.order, bf16[2,1024,128]{2,1,0:T(8,128)(2,1)S(1)} %bitcast.16, bf16[2048,256]{1,0:T(8,128)(2,1)S(1)} %bitcast.18), custom_call_target="tpu_custom_call" | custom-call | flops 2415919104 | bytes 4194304 | tf_op jit(solution)/shard_map/local_share/pallas_call | solution.py:31
  11.4 0.0 collective-permute-done.1.near
  11.4 0.0 copy-start.3
  11.5 0.0 copy-start
  11.5 1.9 %edge_share.1 = (f32[128,3456]{1,0:T(8,128)S(1)}, bf16[128,3456]{1,0:T(8,128)(2,1)S(1)}) custom-call(s32[1]{0:T(128)} %bitcast.core, bf16[1024,128]{1,0:T(8,128)(2,1)S(1)} %collective-permute-done.1.near, bf16[1024,128]{1,0:T(8,128)(2,1)S(1)} %collective-permute-done.far, bf16[256,2048]{1,0:T(8,128)(2,1)S(1)} %get-tuple-element.29.turned, ...), custom_call_target="tpu_custom_call" | custom-call | flops 1207959552 | bytes 4194304 | tf_op jit(solution)/shard_map/edge_share/pallas_call | solution.py:31
  13.5 0.2 collective-permute-start.2
  13.6 0.5 turn_weight.1.turned
  14.2 1.2 %copy-done.1 = bf16[2304,384]{1,0:T(8,128)(2,1)} copy-done((bf16[2304,384]{1,0:T(8,128)(2,1)}, bf16[2304,384]{1,0:T(8,128)(2,1)S(1)}, u32[]{:S(2)}) %copy-start.1) | copy-done | bytes 1769496
  15.4 0.6 collective-permute-done.2
  16.0 1.1 %fusion = bf16[16,8,3456]{2,1,0:T(8,128)(2,1)} fusion(f32[128,3456]{1,0:T(8,128)S(1)} %get-tuple-element.31, bf16[128,3456]{1,0:T(8,128)(2,1)S(1)} %collective-permute-done.2), kind=kLoop, calls=%fused_computation.2 | loop fusion | flops 1327104 | bytes 3538944 | tf_op jit(solution)/shard_map/reshape | solution.py:243
  17.1 6.8 %all-to-all-start = ((bf16[16,8,3456]{2,1,0:T(8,128)(2,1)}), bf16[16,8,3456]{2,1,0:T(8,128)(2,1)S(1)}, u32[]{:S(2)}, u32[]{:S(2)}) async-start(bf16[16,8,3456]{2,1,0:T(8,128)(2,1)} %fusion), calls=%async_computation | async-start | bytes 1769472 | tf_op jit(solution)/shard_map/all_to_all | solution.py:244
  23.9 0.2 collective-permute-start.3
  24.0 2.0 %collective-permute-start.4 = (bf16[1024,256]{1,0:T(8,128)(2,1)S(1)}, bf16[1024,256]{1,0:T(8,128)(2,1)S(1)}, u32[]{:S(2)}, u32[]{:S(2)}) collective-permute-start(bf16[1024,256]{1,0:T(8,128)(2,1)S(1)} %get-tuple-element.42), channel_id=1, source_target_pairs={{1,2},{2,1},{3,4},{4,3},{5,6},{6,5},{7,8},{8,7},{9,10},{10,9},{11,... | collective-permute-start | bytes 1572872 | tf_op jit(solution)/shard_map/ppermute | solution.py:206
  26.1 7.5 %forward.1 = bf16[2048,256]{1,0:T(8,128)(2,1)} custom-call(s32[1]{0:T(128)} %bitcast.core, bf16[1024,128]{1,0:T(8,128)(2,1)} %copy-done.3, bf16[2,1024,128]{2,1,0:T(8,128)(2,1)} %bitcast.15, bf16[1024,128]{1,0:T(8,128)(2,1)} %copy-done.4, bf16[3456,256]{1,0:T(8,128)(2,1)} %bitcast.12), custom_call_target="tpu_custom_call" | custom-call | flops 3623878656 | bytes 4194304 | tf_op jit(solution)/shard_map/forward/pallas_call | solution.py:31
  33.5 6.7 %all-to-all-done = bf16[16,8,3456]{2,1,0:T(8,128)(2,1)S(1)} async-done(((bf16[16,8,3456]{2,1,0:T(8,128)(2,1)}), bf16[16,8,3456]{2,1,0:T(8,128)(2,1)S(1)}, u32[]{:S(2)}, u32[]{:S(2)}) %all-to-all-start) | async-done | bytes 884768 | tf_op jit(solution)/shard_map/all_to_all | solution.py:244
  40.2 0.1 convert_reduce_fusion
  40.3 0.7 %reshape.56 = f32[8,1,3456]{2,1,0:T(1,128)} reshape(f32[8,3456]{1,0:T(8,128)S(1)} %convert_reduce_fusion) | data formatting | bytes 221184 | tf_op jit(solution)/shard_map/reshape | solution.py:248
  41.0 7.8 %all-to-all-start.1 = ((f32[8,1,3456]{2,1,0:T(1,128)}), f32[8,1,3456]{2,1,0:T(1,128)S(1)}, u32[]{:S(2)}, u32[]{:S(2)}) async-start(f32[8,1,3456]{2,1,0:T(1,128)} %reshape.56), calls=%async_computation.1 | async-start | bytes 221184 | tf_op jit(solution)/shard_map/all_to_all | solution.py:250
  48.9 0.0 collective-permute-done.3.near
  48.9 0.8 %copy-done.6 = bf16[1024,256]{1,0:T(8,128)(2,1)} copy-done((bf16[1024,256]{1,0:T(8,128)(2,1)}, bf16[1024,256]{1,0:T(8,128)(2,1)S(1)}, u32[]{:S(2)}) %copy-start.6) | copy-done | bytes 524312
  49.7 0.8 %copy-done.7 = bf16[1024,256]{1,0:T(8,128)(2,1)} copy-done((bf16[1024,256]{1,0:T(8,128)(2,1)}, bf16[1024,256]{1,0:T(8,128)(2,1)S(1)}, u32[]{:S(2)}) %copy-start.7) | copy-done | bytes 524312
  50.5 8.2 %input_grad.1 = bf16[2048,128]{1,0:T(8,128)(2,1)} custom-call(s32[1]{0:T(128)} %bitcast.core, bf16[1024,256]{1,0:T(8,128)(2,1)} %copy-done.6, bf16[2048,256]{1,0:T(8,128)(2,1)} %bitcast.17, bf16[1024,256]{1,0:T(8,128)(2,1)} %copy-done.7, bf16[2304,384]{1,0:T(8,128)(2,1)} %copy-done.1), custom_call_target="tpu_custom_call" | custom-call | flops 3623878656 | bytes 4194304 | tf_op jit(solution)/shard_map/input_grad/pallas_call | solution.py:31
  58.7 0.0 all-to-all-done.1
  58.7 0.1 reduce_sum.19
  58.8 0.6 %div.10 = f32[1,3456]{1,0:T(1,128)} reshape(f32[3456]{0:T(1024)S(1)} %broadcast_multiply_fusion) | data formatting | bytes 27648 | tf_op jit(solution)/shard_map/div | solution.py:258
  (12 shorter events, 0.0 us)
Async XLA Ops:
  1.7 9.7 %collective-permute-start.1 = (bf16[1024,128]{1,0:T(8,128)(2,1)S(1)}, bf16[1024,128]{1,0:T(8,128)(2,1)S(1)}, u32[]{:S(2)}, u32[]{:S(2)}) collective-permute-start(bf16[1024,128]{1,0:T(8,128)(2,1)S(1)} %get-tuple-element.47), channel_id=1, source_target_pairs={{0,1},{1,0},{2,3},{3,2},{4,5},{5,4},{6,7},{7,6},{8,9},{9,8},{10,11... | collective-permute-start | bytes 786440 | tf_op jit(solution)/shard_map/ppermute | solution.py:202
  1.8 9.6 %collective-permute-start = (bf16[1024,128]{1,0:T(8,128)(2,1)S(1)}, bf16[1024,128]{1,0:T(8,128)(2,1)S(1)}, u32[]{:S(2)}, u32[]{:S(2)}) collective-permute-start(bf16[1024,128]{1,0:T(8,128)(2,1)S(1)} %get-tuple-element.48), channel_id=1, source_target_pairs={{1,2},{2,1},{3,4},{4,3},{5,6},{6,5},{7,8},{8,7},{9,10},{10,9},{11,... | collective-permute-start | bytes 786440 | tf_op jit(solution)/shard_map/ppermute | solution.py:206
  5.8 1.0 %copy-start.2 = (bf16[1,2,32,32,128]{4,3,2,1,0:T(8,128)(2,1)S(1)}, bf16[1,2,32,32,128]{4,3,2,1,0:T(8,128)(2,1)}, u32[]{:S(2)}) copy-start(bf16[1,2,32,32,128]{4,3,2,1,0:T(8,128)(2,1)} %param.3) | copy-start | bytes 1572868
  6.8 1.2 %copy-start.5 = (bf16[1,2,32,32,256]{4,3,2,1,0:T(8,128)(2,1)S(1)}, bf16[1,2,32,32,256]{4,3,2,1,0:T(8,128)(2,1)}, u32[]{:S(2)}) copy-start(bf16[1,2,32,32,256]{4,3,2,1,0:T(8,128)(2,1)} %param.5) | copy-start | bytes 3145732
  11.4 2.0 %copy-start.3 = (bf16[1024,128]{1,0:T(8,128)(2,1)}, bf16[1024,128]{1,0:T(8,128)(2,1)S(1)}, u32[]{:S(2)}) copy-start(bf16[1024,128]{1,0:T(8,128)(2,1)S(1)} %collective-permute-done.1.near) | copy-start | bytes 786436
  11.5 2.0 %copy-start.4 = (bf16[1024,128]{1,0:T(8,128)(2,1)}, bf16[1024,128]{1,0:T(8,128)(2,1)S(1)}, u32[]{:S(2)}) copy-start(bf16[1024,128]{1,0:T(8,128)(2,1)S(1)} %collective-permute-done.far) | copy-start | bytes 786436
  11.5 2.2 %copy-start = (bf16[27,128,256]{2,1,0:T(8,128)(2,1)S(1)}, bf16[27,128,256]{2,1,0:T(8,128)(2,1)}, u32[]{:S(2)}) copy-start(bf16[27,128,256]{2,1,0:T(8,128)(2,1)} %param.4) | copy-start | bytes 5308420
  13.5 2.5 %collective-permute-start.2 = (bf16[128,3456]{1,0:T(8,128)(2,1)S(1)}, bf16[128,3456]{1,0:T(8,128)(2,1)S(1)}, u32[]{:S(2)}, u32[]{:S(2)}) collective-permute-start(bf16[128,3456]{1,0:T(8,128)(2,1)S(1)} %get-tuple-element.32), channel_id=1, source_target_pairs={{0,1},{1,0},{2,3},{3,2},{4,5},{5,4},{6,7},{7,6},{8,9},{9,8},{10,11... | collective-permute-start | bytes 2654216 | tf_op jit(solution)/shard_map/ppermute | solution.py:202
  14.2 1.2 %copy-start.1 = (bf16[2304,384]{1,0:T(8,128)(2,1)}, bf16[2304,384]{1,0:T(8,128)(2,1)S(1)}, u32[]{:S(2)}) copy-start(bf16[2304,384]{1,0:T(8,128)(2,1)S(1)} %turn_weight.1.turned) | copy-start | bytes 5308420
  17.1 23.1 %all-to-all-start = ((bf16[16,8,3456]{2,1,0:T(8,128)(2,1)}), bf16[16,8,3456]{2,1,0:T(8,128)(2,1)S(1)}, u32[]{:S(2)}, u32[]{:S(2)}) async-start(bf16[16,8,3456]{2,1,0:T(8,128)(2,1)} %fusion), calls=%async_computation | async-start | bytes 1769472 | tf_op jit(solution)/shard_map/all_to_all | solution.py:244
  23.9 25.0 %collective-permute-start.3 = (bf16[1024,256]{1,0:T(8,128)(2,1)S(1)}, bf16[1024,256]{1,0:T(8,128)(2,1)S(1)}, u32[]{:S(2)}, u32[]{:S(2)}) collective-permute-start(bf16[1024,256]{1,0:T(8,128)(2,1)S(1)} %get-tuple-element.41), channel_id=1, source_target_pairs={{0,1},{1,0},{2,3},{3,2},{4,5},{5,4},{6,7},{7,6},{8,9},{9,8},{10,11... | collective-permute-start | bytes 1572872 | tf_op jit(solution)/shard_map/ppermute | solution.py:202
  24.0 24.9 %collective-permute-start.4 = (bf16[1024,256]{1,0:T(8,128)(2,1)S(1)}, bf16[1024,256]{1,0:T(8,128)(2,1)S(1)}, u32[]{:S(2)}, u32[]{:S(2)}) collective-permute-start(bf16[1024,256]{1,0:T(8,128)(2,1)S(1)} %get-tuple-element.42), channel_id=1, source_target_pairs={{1,2},{2,1},{3,4},{4,3},{5,6},{6,5},{7,8},{8,7},{9,10},{10,9},{11,... | collective-permute-start | bytes 1572872 | tf_op jit(solution)/shard_map/ppermute | solution.py:206
  41.0 17.6 %all-to-all-start.1 = ((f32[8,1,3456]{2,1,0:T(1,128)}), f32[8,1,3456]{2,1,0:T(1,128)S(1)}, u32[]{:S(2)}, u32[]{:S(2)}) async-start(f32[8,1,3456]{2,1,0:T(1,128)} %reshape.56), calls=%async_computation.1 | async-start | bytes 221184 | tf_op jit(solution)/shard_map/all_to_all | solution.py:250
  48.9 0.8 %copy-start.6 = (bf16[1024,256]{1,0:T(8,128)(2,1)}, bf16[1024,256]{1,0:T(8,128)(2,1)S(1)}, u32[]{:S(2)}) copy-start(bf16[1024,256]{1,0:T(8,128)(2,1)S(1)} %collective-permute-done.3.near) | copy-start | bytes 1572868
  49.7 0.8 %copy-start.7 = (bf16[1024,256]{1,0:T(8,128)(2,1)}, bf16[1024,256]{1,0:T(8,128)(2,1)S(1)}, u32[]{:S(2)}) copy-start(bf16[1024,256]{1,0:T(8,128)(2,1)S(1)} %collective-permute-done.4.far) | copy-start | bytes 1572868

commit v4 on v3

--- a/solution.py
+++ b/solution.py
@@ -1,3 +1,5 @@
+import functools
+
 import jax
 import jax.numpy as jnp
 from jax import lax
@@ -12,7 +14,7 @@
 SLAB = 2
 PADDED = CELLS + 2 * SIDE
 COLUMNS = TAPS * CIN
-VMEM_SOME, VMEM_MOST = 24 << 20, 58 << 20
+VMEM_SOME, VMEM_MORE, VMEM_MOST = 24 << 20, 55_000_000, 63_400_000
 FLOPS = 2 * SLAB * CELLS * TAPS * CIN * COUT
 
 IN_VMEM = pl.BlockSpec(memory_space=pltpu.VMEM)
@@ -118,16 +120,31 @@
     return call(edge_share_kernel, outs, args, taps_scratch(2), FLOPS // 3, name="edge_share")
 
 
-def forward_kernel(core, near, volume, far, weight, out, wide, taps):
+def start_all(pairs, sems):
+    copies = [pltpu.make_async_copy(source, target, sems.at[i]) for i, (source, target) in enumerate(pairs)]
+    for copy in copies:
+        copy.start()
+    return copies
+
+
+def forward_kernel(core, near, volume, far, weight_in_hbm, out, wide, taps, planes, weight, sems):
     c = core[0]
     step = pl.program_id(0)
 
     @pl.when(step == 0)
     def _():
+        own, *outer, whole = start_all(
+            [(volume, planes.at[pl.ds(0, SLAB)]), (near, planes.at[2]), (far, planes.at[3]), (weight_in_hbm, weight)],
+            sems,
+        )
+        own.wait()
         for i in range(SLAB):
-            fill_taps(volume.at[i], 1 + i, wide, taps)
-        fill_taps(near, 3 * (1 - c), wide, taps)
-        fill_taps(far, 3 * c, wide, taps)
+            fill_taps(planes.at[i], 1 + i, wide, taps)
+        for copy in outer:
+            copy.wait()
+        fill_taps(planes.at[2], 3 * (1 - c), wide, taps)
+        fill_taps(planes.at[3], 3 * c, wide, taps)
+        whole.wait()
 
     parts = []
     for k in range(TAPS):
@@ -137,12 +154,18 @@
 
 
 def forward(*args):
+    own_copies = [
+        pltpu.VMEM((4, CELLS, CIN), bf16),
+        pltpu.VMEM((COLUMNS, COUT), bf16),
+        pltpu.SemaphoreType.DMA((4,)),
+    ]
     return call(
         forward_kernel,
         (shaped(bf16, SLAB * CELLS, COUT),),
         args,
-        taps_scratch(4),
+        taps_scratch(4) + own_copies,
         FLOPS,
+        specs=[IN_SMEM] + [IN_HBM] * 4,
         grid=(SLAB,),
         out_specs=(pl.BlockSpec((CELLS, COUT), lambda i: (i, 0)),),
         vmem=VMEM_MOST,
@@ -150,6 +173,29 @@
     )[0]
 
 
+def sum_rows_kernel(parts, rows, spread):
+    total = parts[0].astype(f32)
+    for i in range(1, parts.shape[0]):
+        total = total + parts[i].astype(f32)
+    for k in range(TAPS):
+        spread[:, k, :] = total[:, k * CIN : (k + 1) * CIN]
+    rows[...] = spread[...].astype(bf16)
+
+
+def sum_rows(parts):
+    shape = (parts.shape[1], TAPS, CIN)
+    return call(sum_rows_kernel, (shaped(bf16, *shape),), (parts,), [pltpu.VMEM(shape, f32)], name="sum_rows")[0]
+
+
+def finish(parts, count):
+    def kernel(parts, row):
+        total = jnp.sum(parts[...].astype(f32), axis=0) / jnp.sqrt(f32(count))
+        for k in range(TAPS):
+            row[:, pl.ds(k * CIN, CIN)] = total[k : k + 1, :]
+
+    return call(kernel, (shaped(f32, 1, COLUMNS),), (parts,), name="finish")[0]
+
+
 def turn_weight_kernel(weight, turned):
     for k in range(TAPS):
         turned[pl.ds(k // 3 * COUT, COUT), pl.ds(k % 3 * CIN, CIN)] = weight[pl.ds(k * CIN, CIN), :].T
@@ -159,42 +205,59 @@
     return call(turn_weight_kernel, (shaped(bf16, 9 * COUT, 3 * CIN),), (weight,), name="turn_weight")[0]
 
 
-def input_grad_kernel(core, near, cot, far, turned, out, padded, sums):
-    c = core[0]
-    step = pl.program_id(0)
+def input_grad_kernel(is_far, core, halo, cot, turned, *rest):
+    out, padded, weight, sums, result, sems = rest[-6:]
+    d = core[0] if is_far else 1 - core[0]
     middle = pl.ds(SIDE, CELLS)
-
-    @pl.when(step == 0)
-    def _():
-        zero = jnp.zeros((SIDE, COUT), bf16)
-        for i in range(4):
-            padded[i, pl.ds(0, SIDE), :] = zero
-            padded[i, pl.ds(SIDE + CELLS, SIDE), :] = zero
-        for i in range(SLAB):
-            padded[1 + i, middle, :] = cot[pl.ds(i * CELLS, CELLS), :]
-        padded[3 * (1 - c), middle, :] = near[...]
-        padded[3 * c, middle, :] = far[...]
-
-    parts = [padded[step + 2 - j // 3, pl.ds((2 - j % 3) * SIDE, CELLS), :] for j in range(9)]
-    sums[pl.ds(8, CELLS), :] = product(jnp.concatenate(parts, axis=1), turned[...])
+    planes = [
+        cot.at[pl.ds(pl.multiple_of(d * CELLS, CELLS), CELLS)],
+        cot.at[pl.ds(pl.multiple_of((1 - d) * CELLS, CELLS), CELLS)],
+        halo,
+    ]
+    pairs = []
+    for slot, kd in enumerate((1, 2 * d, 2 - 2 * d)):
+        rows = pl.ds(pl.multiple_of(kd * 3 * COUT, 3 * COUT), 3 * COUT)
+        pairs += [(planes[slot], padded.at[slot, middle]), (turned.at[rows], weight.at[slot])]
+    copies = start_all(pairs, sems)
+    zero = jnp.zeros((SIDE, COUT), bf16)
+    inner = pl.ds(8, CELLS)
+    for slot in range(3):
+        padded[slot, pl.ds(0, SIDE), :] = zero
+        padded[slot, pl.ds(SIDE + CELLS, SIDE), :] = zero
+        for copy in copies[2 * slot : 2 * slot + 2]:
+            copy.wait()
+        parts = [padded[slot, pl.ds((2 - kh) * SIDE, CELLS), :] for kh in range(3)]
+        part = product(jnp.concatenate(parts, axis=1), weight[slot])
+        sums[inner, :] = part if slot == 0 else sums[inner, :] + part
     col = lax.broadcasted_iota(jnp.int32, (CELLS, CIN), 0) % SIDE
-    total = sums[pl.ds(8, CELLS), pl.ds(CIN, CIN)]
+    total = sums[inner, pl.ds(CIN, CIN)]
     total = total + jnp.where(col < SIDE - 1, sums[pl.ds(9, CELLS), pl.ds(0, CIN)], 0.0)
     total = total + jnp.where(col > 0, sums[pl.ds(7, CELLS), pl.ds(2 * CIN, CIN)], 0.0)
-    out[...] = total.astype(bf16)
-
-
-def input_grad_of(*args):
+    result[...] = total.astype(bf16)
+    write = pltpu.make_async_copy(result, out.at[pl.ds(pl.multiple_of(d * CELLS, CELLS), CELLS)], sems.at[6])
+    write.start()
+    write.wait()
+
+
+def input_grad_plane(is_far, *args):
+    scratch = [
+        pltpu.VMEM((3, PADDED, COUT), bf16),
+        pltpu.VMEM((3, 3 * COUT, 3 * CIN), bf16),
+        pltpu.VMEM((CELLS + 16, 3 * CIN), f32),
+        pltpu.VMEM((CELLS, CIN), bf16),
+        pltpu.SemaphoreType.DMA((7,)),
+    ]
     return call(
-        input_grad_kernel,
+        functools.partial(input_grad_kernel, is_far),
         (shaped(bf16, SLAB * CELLS, CIN),),
         args,
-        [pltpu.VMEM((4, PADDED, COUT), bf16), pltpu.VMEM((CELLS + 16, 3 * CIN), f32)],
-        FLOPS,
-        grid=(SLAB,),
-        out_specs=(pl.BlockSpec((CELLS, CIN), lambda i: (i, 0)),),
-        vmem=VMEM_MOST,
-        name="input_grad",
+        scratch,
+        FLOPS // 2,
+        specs=[IN_SMEM] + [IN_HBM] * (len(args) - 1),
+        out_specs=(IN_HBM,),
+        input_output_aliases={4: 0} if len(args) > 4 else {},
+        vmem=VMEM_MORE,
+        name="input_grad_far" if is_far else "input_grad_near",
     )[0]
 
 
@@ -206,10 +269,14 @@
     return lax.ppermute(value, "space", [(i, ((i + 1) ^ 1) - 1) for i in range(1, 15)])
 
 
+def row_order_kernel(core, order):
+    place = lax.broadcasted_iota(jnp.int32, (COUT, COUT), 0)
+    row = (place & 127) * 2 + (core[0] ^ (place >> 7))
+    order[...] = jnp.where(row == lax.broadcasted_iota(jnp.int32, (COUT, COUT), 1), 1.0, 0.0).astype(bf16)
+
+
 def row_order(core):
-    place = lax.iota(jnp.int32, COUT)
-    row = (place & 127) * 2 + (core ^ (place >> 7))
-    return (row[:, None] == lax.iota(jnp.int32, COUT)[None, :]).astype(bf16)
+    return call(row_order_kernel, (shaped(bf16, COUT, COUT),), (core,), flops=FLOPS, name="row_order")[0]
 
 
 def together(*arrays):
@@ -226,8 +293,9 @@
     def plane(i):
         return lax.dynamic_index_in_dim(volume, i, 0, False)
 
-    far, near = from_chip(plane(core)), from_core(plane(1 - core))
-    cot_near, cot_far, turned, share = local_share(flag, row_order(core), volume, cot)
+    far, near, order = together(plane(core), plane(1 - core), row_order(flag))
+    far, near = from_chip(far), from_core(near)
+    cot_near, cot_far, turned, share = local_share(flag, order, volume, cot)
     far, near, turned, share = together(far, near, turned, share)
     keep, send = edge_share(flag, near, far, turned, share)
 
@@ -244,18 +312,20 @@
     parts = lax.all_to_all(send, "dp", 0, 0)
     weight, send = together(weight, send)
     activation = forward(flag, near, volume, far, weight)
-    parts, activation = together(parts, activation)
-    send = jnp.sum(parts.astype(f32), axis=0).reshape(8, 1, COLUMNS)
+    back_weight, activation = together(back_weight, activation)
+    input_grad = input_grad_plane(False, flag, cot_near, cot, back_weight)
+    parts, input_grad = together(parts, input_grad)
+    send = sum_rows(parts)
 
     parts = lax.all_to_all(send, "space", 0, 0, axis_index_groups=[list(range(c, 16, 2)) for c in range(2)])
     back_weight, send = together(back_weight, send)
-    input_grad = input_grad_of(flag, cot_near, cot, cot_far, back_weight)
+    input_grad = input_grad_plane(True, flag, cot_far, cot, back_weight, input_grad)
     parts, input_grad = together(parts, input_grad)
     count = dp * lax.axis_size("space") * SLAB * CELLS
     return (
         activation.reshape(1, SLAB, SIDE, SIDE, COUT),
         input_grad.reshape(1, SLAB, SIDE, SIDE, CIN),
-        jnp.sum(parts, axis=0) / jnp.sqrt(f32(count)),
+        finish(parts, count),
     )
 
 

time: 59.8 us -> 57.2 us (0.957)
  the two profiles are of different devices: /device:TPU:32 before, /device:TPU:6 now
where the time goes in v4:
time: 57.2 us; the launch traced here: 56.3 us
  Pallas kernels  23.5 us (41%)
  starting transfers between devices  22.3 us (39%)
  waiting for transfers between devices  5.63 us (10%)
  local copies, waits for them, and re-layouts  3.04 us (5%)
  other arithmetic  1.05 us (2%)
  between operations  0.84 us (1%)
    pallas_call x9, Pallas kernels, call(): pl.pallas_call(kernel, out_shape=outs, in_specs=specs, scratch_shapes=lis...  23.5 us
    all_to_all x1, starting transfers between devices, shards(): lax.all_to_all(send, 'space', 0, 0, axis_index_groups=[list(range(c, 16,...  9.78 us
    all_to_all x1, starting transfers between devices, shards(): parts = lax.all_to_all(send, 'dp', 0, 0)  7.56 us
    all_to_all x1, waiting for transfers between devices, shards(): lax.all_to_all(send, 'space', 0, 0, axis_index_groups=[list(range(c, 16,...  3.67 us
    ppermute x3, starting transfers between devices, from_core(): return lax.ppermute(value, 'space', [(i, i ^ 1) for i in range(16)])  3.55 us
    unnamed x20, local copies, waits for them, and re-layouts  3.01 us
    ppermute x2, starting transfers between devices, from_chip(): lax.ppermute(value, 'space', [(i, (i + 1 ^ 1) - 1) for i in range(1, 15)])  1.37 us
    all_to_all x1, waiting for transfers between devices, shards(): parts = lax.all_to_all(send, 'dp', 0, 0)  1.31 us
  transfers between devices with their start and end apart: 7, of which 3 were waited for; matrix products, arithmetic and copies ran while one was open for 0% of the time, Pallas kernels for 37%

profile of v4, /device:TPU:6, one launch (start us, length us, event | category | flops | bytes accessed | tf_op | source)
XLA Modules:
  0.0 56.3 jit_solution(4910454544604818768)
XLA Ops:
  0.6 0.0 copy-start.2
  0.7 0.0 copy-start.5
  0.7 0.1 row_order.1.order
  0.7 0.9 %copy-done.2 = bf16[1,2,32,32,128]{4,3,2,1,0:T(8,128)(2,1)S(1)} copy-done((bf16[1,2,32,32,128]{4,3,2,1,0:T(8,128)(2,1)S(1)}, bf16[1,2,32,32,128]{4,3,2,1,0:T(8,128)(2,1)}, u32[]{:S(2)}) %copy-start.2) | copy-done | bytes 524312
  1.7 0.7 %collective-permute-start = (bf16[1024,128]{1,0:T(8,128)(2,1)S(1)}, bf16[1024,128]{1,0:T(8,128)(2,1)S(1)}, u32[]{:S(2)}, u32[]{:S(2)}) collective-permute-start(bf16[1024,128]{1,0:T(8,128)(2,1)S(1)} %get-tuple-element.30), channel_id=1, source_target_pairs={{1,2},{2,1},{3,4},{4,3},{5,6},{6,5},{7,8},{8,7},{9,10},{10,9},{11,... | collective-permute-start | bytes 786440 | tf_op jit(solution)/shard_map/ppermute | solution.py:269
  2.4 3.4 %collective-permute-start.1 = (bf16[1024,128]{1,0:T(8,128)(2,1)S(1)}, bf16[1024,128]{1,0:T(8,128)(2,1)S(1)}, u32[]{:S(2)}, u32[]{:S(2)}) collective-permute-start(bf16[1024,128]{1,0:T(8,128)(2,1)S(1)} %get-tuple-element.31), channel_id=1, source_target_pairs={{0,1},{1,0},{2,3},{3,2},{4,5},{5,4},{6,7},{7,6},{8,9},{9,8},{10,11... | collective-permute-start | bytes 786440 | tf_op jit(solution)/shard_map/ppermute | solution.py:265
  5.8 3.3 %local_share.1 = (bf16[1024,256]{1,0:T(8,128)(2,1)S(1)}, bf16[1024,256]{1,0:T(8,128)(2,1)S(1)}, bf16[256,2048]{1,0:T(8,128)(2,1)S(1)}, f32[256,3456]{1,0:T(8,128)S(1)}) custom-call(s32[1]{0:T(128)} %bitcast.core, bf16[256,256]{1,0:T(8,128)(2,1)S(1)} %row_order.1.order, bf16[2,1024,128]{2,1,0:T(8,128)(2,1)S(1)} %bitcast.16, bf16[2048,256]{1,0:T(8,128)(2,1)S(1)} %bitcast.19), custom_call_target="tpu_custom_call" | custom-call | flops 2415919104 | bytes 4194304 | tf_op jit(solution)/shard_map/local_share/pallas_call | solution.py:33
  9.1 0.0 copy-start.8
  9.1 0.8 %copy-done.8 = bf16[1024,256]{1,0:T(8,128)(2,1)} copy-done((bf16[1024,256]{1,0:T(8,128)(2,1)}, bf16[1024,256]{1,0:T(8,128)(2,1)S(1)}, u32[]{:S(2)}) %copy-start.8) | copy-done | bytes 524312
  9.9 0.0 collective-permute-done.far
  9.9 0.0 collective-permute-done.1.near
  9.9 0.0 copy-start
  9.9 1.9 %edge_share.1 = (f32[128,3456]{1,0:T(8,128)S(1)}, bf16[128,3456]{1,0:T(8,128)(2,1)S(1)}) custom-call(s32[1]{0:T(128)} %bitcast.core, bf16[1024,128]{1,0:T(8,128)(2,1)S(1)} %collective-permute-done.1.near, bf16[1024,128]{1,0:T(8,128)(2,1)S(1)} %collective-permute-done.far, bf16[256,2048]{1,0:T(8,128)(2,1)S(1)} %get-tuple-element.37.turned, ...), custom_call_target="tpu_custom_call" | custom-call | flops 1207959552 | bytes 4194304 | tf_op jit(solution)/shard_map/edge_share/pallas_call | solution.py:33
  11.9 0.1 collective-permute-start.2
  12.0 0.0 copy-done
  12.0 0.5 turn_weight.1.turned
  12.5 1.2 %copy-done.1 = bf16[2304,384]{1,0:T(8,128)(2,1)} copy-done((bf16[2304,384]{1,0:T(8,128)(2,1)}, bf16[2304,384]{1,0:T(8,128)(2,1)S(1)}, u32[]{:S(2)}) %copy-start.1) | copy-done | bytes 1769496
  13.8 0.6 %collective-permute-done.2 = bf16[128,3456]{1,0:T(8,128)(2,1)S(1)} collective-permute-done((bf16[128,3456]{1,0:T(8,128)(2,1)S(1)}, bf16[128,3456]{1,0:T(8,128)(2,1)S(1)}, u32[]{:S(2)}, u32[]{:S(2)}) %collective-permute-start.2) | collective-permute-done | bytes 884768 | tf_op jit(solution)/shard_map/ppermute | solution.py:265
  14.4 1.1 %fusion = bf16[16,8,3456]{2,1,0:T(8,128)(2,1)} fusion(f32[128,3456]{1,0:T(8,128)S(1)} %get-tuple-element.45, bf16[128,3456]{1,0:T(8,128)(2,1)S(1)} %collective-permute-done.2), kind=kLoop, calls=%fused_computation.1 | loop fusion | flops 1327104 | bytes 3538944 | tf_op jit(solution)/shard_map/reshape | solution.py:311
  15.5 7.6 %all-to-all-start = ((bf16[16,8,3456]{2,1,0:T(8,128)(2,1)}), bf16[16,8,3456]{2,1,0:T(8,128)(2,1)S(1)}, u32[]{:S(2)}, u32[]{:S(2)}) async-start(bf16[16,8,3456]{2,1,0:T(8,128)(2,1)} %fusion), calls=%async_computation | async-start | bytes 1769472 | tf_op jit(solution)/shard_map/all_to_all | solution.py:312
  23.0 0.1 collective-permute-start.3
  23.2 0.7 %collective-permute-start.4 = (bf16[1024,256]{1,0:T(8,128)(2,1)S(1)}, bf16[1024,256]{1,0:T(8,128)(2,1)S(1)}, u32[]{:S(2)}, u32[]{:S(2)}) collective-permute-start(bf16[1024,256]{1,0:T(8,128)(2,1)S(1)} %copy-done.7), channel_id=1, source_target_pairs={{1,2},{2,1},{3,4},{4,3},{5,6},{6,5},{7,8},{8,7},{9,10},{10,9},{11,... | collective-permute-start | bytes 1572872 | tf_op jit(solution)/shard_map/ppermute | solution.py:269
  23.9 6.8 %forward.1 = bf16[2048,256]{1,0:T(8,128)(2,1)} custom-call(s32[1]{0:T(128)} %bitcast.core, bf16[1024,128]{1,0:T(8,128)(2,1)} %copy-done.4, bf16[2,1024,128]{2,1,0:T(8,128)(2,1)} %bitcast.14, bf16[1024,128]{1,0:T(8,128)(2,1)} %copy-done.3, bf16[3456,256]{1,0:T(8,128)(2,1)} %bitcast.12), custom_call_target="tpu_custom_call" | custom-call | flops 3623878656 | bytes 4194304 | tf_op jit(solution)/shard_map/forward/pallas_call | solution.py:33
  30.7 0.0 collective-permute-done.3.halo
  30.7 4.7 %input_grad_near.1.rest_0_ = bf16[2048,128]{1,0:T(8,128)(2,1)} custom-call(s32[1]{0:T(128)} %bitcast.core, bf16[1024,256]{1,0:T(8,128)(2,1)S(1)} %collective-permute-done.3.halo, bf16[2048,256]{1,0:T(8,128)(2,1)} %bitcast.17, bf16[2304,384]{1,0:T(8,128)(2,1)} %copy-done.1), custom_call_target="tpu_custom_call" | custom-call | flops 1811939328 | bytes 4194304 | tf_op jit(solution)/shard_map/input_grad_near/pallas_call | solution.py:33
  35.4 1.3 %all-to-all-done.parts = bf16[16,8,3456]{2,1,0:T(8,128)(2,1)S(1)} async-done(((bf16[16,8,3456]{2,1,0:T(8,128)(2,1)}), bf16[16,8,3456]{2,1,0:T(8,128)(2,1)S(1)}, u32[]{:S(2)}, u32[]{:S(2)}) %all-to-all-start) | async-done | bytes 884768 | tf_op jit(solution)/shard_map/all_to_all | solution.py:312
  36.7 0.8 %sum_rows.1 = bf16[8,27,128]{2,1,0:T(8,128)(2,1)} custom-call(bf16[16,8,3456]{2,1,0:T(8,128)(2,1)S(1)} %all-to-all-done.parts), custom_call_target="tpu_custom_call" | custom-call | flops 1048576 | bytes 4194304 | tf_op jit(solution)/shard_map/sum_rows/pallas_call | solution.py:33
  37.5 9.8 %all-to-all-start.1 = ((bf16[8,27,128]{2,1,0:T(8,128)(2,1)}), bf16[8,27,128]{2,1,0:T(8,128)(2,1)S(1)}, u32[]{:S(2)}, u32[]{:S(2)}) async-start(bf16[8,27,128]{2,1,0:T(8,128)(2,1)} %sum_rows.1), calls=%async_computation.1 | async-start | bytes 131072 | tf_op jit(solution)/shard_map/all_to_all | solution.py:320
  47.3 0.0 collective-permute-done.4.halo
  47.3 4.7 %input_grad_far.1 = bf16[2048,128]{1,0:T(8,128)(2,1)} custom-call(s32[1]{0:T(128)} %bitcast.core, bf16[1024,256]{1,0:T(8,128)(2,1)S(1)} %collective-permute-done.4.halo, bf16[2048,256]{1,0:T(8,128)(2,1)} %bitcast.18, bf16[2304,384]{1,0:T(8,128)(2,1)} %copy-done.1, bf16[2048,128]{1,0:T(8,128)(2,1)} %input_grad_near.1.rest_0_), custom_call_target="tpu_custom_call", output_to_operand_aliasing={{}: (4, {})} | custom-call | flops 1811939328 | bytes 4194304 | tf_op jit(solution)/shard_map/input_grad_far/pallas_call | solution.py:33
  52.0 3.7 %all-to-all-done.1.parts = bf16[8,27,128]{2,1,0:T(8,128)(2,1)S(1)} async-done(((bf16[8,27,128]{2,1,0:T(8,128)(2,1)}), bf16[8,27,128]{2,1,0:T(8,128)(2,1)S(1)}, u32[]{:S(2)}, u32[]{:S(2)}) %all-to-all-start.1) | async-done | bytes 55328 | tf_op jit(solution)/shard_map/all_to_all | solution.py:320
  55.7 0.6 %finish.1 = f32[1,3456]{1,0:T(1,128)} custom-call(bf16[8,27,128]{2,1,0:T(8,128)(2,1)S(1)} %all-to-all-done.1.parts), custom_call_target="tpu_custom_call" | custom-call | flops 1048576 | bytes 4194304 | tf_op jit(solution)/shard_map/finish/pallas_call | solution.py:33
  (13 shorter events, 0.1 us)
Async XLA Ops:
  0.6 1.0 %copy-start.2 = (bf16[1,2,32,32,128]{4,3,2,1,0:T(8,128)(2,1)S(1)}, bf16[1,2,32,32,128]{4,3,2,1,0:T(8,128)(2,1)}, u32[]{:S(2)}) copy-start(bf16[1,2,32,32,128]{4,3,2,1,0:T(8,128)(2,1)} %param.3) | copy-start | bytes 1572868
  0.7 5.1 %copy-start.5 = (bf16[1,2,32,32,256]{4,3,2,1,0:T(8,128)(2,1)S(1)}, bf16[1,2,32,32,256]{4,3,2,1,0:T(8,128)(2,1)}, u32[]{:S(2)}) copy-start(bf16[1,2,32,32,256]{4,3,2,1,0:T(8,128)(2,1)} %param.5) | copy-start | bytes 3145732
  1.7 8.2 %collective-permute-start = (bf16[1024,128]{1,0:T(8,128)(2,1)S(1)}, bf16[1024,128]{1,0:T(8,128)(2,1)S(1)}, u32[]{:S(2)}, u32[]{:S(2)}) collective-permute-start(bf16[1024,128]{1,0:T(8,128)(2,1)S(1)} %get-tuple-element.30), channel_id=1, source_target_pairs={{1,2},{2,1},{3,4},{4,3},{5,6},{6,5},{7,8},{8,7},{9,10},{10,9},{11,... | collective-permute-start | bytes 786440 | tf_op jit(solution)/shard_map/ppermute | solution.py:269
  2.4 7.5 %collective-permute-start.1 = (bf16[1024,128]{1,0:T(8,128)(2,1)S(1)}, bf16[1024,128]{1,0:T(8,128)(2,1)S(1)}, u32[]{:S(2)}, u32[]{:S(2)}) collective-permute-start(bf16[1024,128]{1,0:T(8,128)(2,1)S(1)} %get-tuple-element.31), channel_id=1, source_target_pairs={{0,1},{1,0},{2,3},{3,2},{4,5},{5,4},{6,7},{7,6},{8,9},{9,8},{10,11... | collective-permute-start | bytes 786440 | tf_op jit(solution)/shard_map/ppermute | solution.py:265
  9.1 0.8 %copy-start.8 = (bf16[1024,256]{1,0:T(8,128)(2,1)}, bf16[1024,256]{1,0:T(8,128)(2,1)S(1)}, u32[]{:S(2)}) copy-start(bf16[1024,256]{1,0:T(8,128)(2,1)S(1)} %get-tuple-element.49) | copy-start | bytes 1572868
  9.9 2.0 %copy-start.6 = (bf16[1024,256]{1,0:T(8,128)(2,1)}, bf16[1024,256]{1,0:T(8,128)(2,1)S(1)}, u32[]{:S(2)}) copy-start(bf16[1024,256]{1,0:T(8,128)(2,1)S(1)} %get-tuple-element.52) | copy-start | bytes 1572868
  9.9 2.0 %copy-start.3 = (bf16[1024,128]{1,0:T(8,128)(2,1)}, bf16[1024,128]{1,0:T(8,128)(2,1)S(1)}, u32[]{:S(2)}) copy-start(bf16[1024,128]{1,0:T(8,128)(2,1)S(1)} %collective-permute-done.far) | copy-start | bytes 786436
  9.9 2.0 %copy-start.4 = (bf16[1024,128]{1,0:T(8,128)(2,1)}, bf16[1024,128]{1,0:T(8,128)(2,1)S(1)}, u32[]{:S(2)}) copy-start(bf16[1024,128]{1,0:T(8,128)(2,1)S(1)} %collective-permute-done.1.near) | copy-start | bytes 786436
  9.9 2.1 %copy-start = (bf16[27,128,256]{2,1,0:T(8,128)(2,1)S(1)}, bf16[27,128,256]{2,1,0:T(8,128)(2,1)}, u32[]{:S(2)}) copy-start(bf16[27,128,256]{2,1,0:T(8,128)(2,1)} %param.4) | copy-start | bytes 5308420
  11.9 2.5 %collective-permute-start.2 = (bf16[128,3456]{1,0:T(8,128)(2,1)S(1)}, bf16[128,3456]{1,0:T(8,128)(2,1)S(1)}, u32[]{:S(2)}, u32[]{:S(2)}) collective-permute-start(bf16[128,3456]{1,0:T(8,128)(2,1)S(1)} %get-tuple-element.39), channel_id=1, source_target_pairs={{0,1},{1,0},{2,3},{3,2},{4,5},{5,4},{6,7},{7,6},{8,9},{9,8},{10,11... | collective-permute-start | bytes 2654216 | tf_op jit(solution)/shard_map/ppermute | solution.py:265
  12.5 1.2 %copy-start.1 = (bf16[2304,384]{1,0:T(8,128)(2,1)}, bf16[2304,384]{1,0:T(8,128)(2,1)S(1)}, u32[]{:S(2)}) copy-start(bf16[2304,384]{1,0:T(8,128)(2,1)S(1)} %turn_weight.1.turned) | copy-start | bytes 5308420
  15.5 7.6 %copy-start.9 = (bf16[1024,256]{1,0:T(8,128)(2,1)S(1)}, bf16[1024,256]{1,0:T(8,128)(2,1)}, u32[]{:S(2)}) copy-start(bf16[1024,256]{1,0:T(8,128)(2,1)} %copy-done.8) | copy-start | bytes 1572868
  15.5 7.7 %copy-start.7 = (bf16[1024,256]{1,0:T(8,128)(2,1)S(1)}, bf16[1024,256]{1,0:T(8,128)(2,1)}, u32[]{:S(2)}) copy-start(bf16[1024,256]{1,0:T(8,128)(2,1)} %copy-done.6) | copy-start | bytes 1572868
  15.5 21.2 %all-to-all-start = ((bf16[16,8,3456]{2,1,0:T(8,128)(2,1)}), bf16[16,8,3456]{2,1,0:T(8,128)(2,1)S(1)}, u32[]{:S(2)}, u32[]{:S(2)}) async-start(bf16[16,8,3456]{2,1,0:T(8,128)(2,1)} %fusion), calls=%async_computation | async-start | bytes 1769472 | tf_op jit(solution)/shard_map/all_to_all | solution.py:312
  23.0 7.6 %collective-permute-start.3 = (bf16[1024,256]{1,0:T(8,128)(2,1)S(1)}, bf16[1024,256]{1,0:T(8,128)(2,1)S(1)}, u32[]{:S(2)}, u32[]{:S(2)}) collective-permute-start(bf16[1024,256]{1,0:T(8,128)(2,1)S(1)} %copy-done.9), channel_id=1, source_target_pairs={{0,1},{1,0},{2,3},{3,2},{4,5},{5,4},{6,7},{7,6},{8,9},{9,8},{10,11... | collective-permute-start | bytes 1572872 | tf_op jit(solution)/shard_map/ppermute | solution.py:265
  23.2 24.2 %collective-permute-start.4 = (bf16[1024,256]{1,0:T(8,128)(2,1)S(1)}, bf16[1024,256]{1,0:T(8,128)(2,1)S(1)}, u32[]{:S(2)}, u32[]{:S(2)}) collective-permute-start(bf16[1024,256]{1,0:T(8,128)(2,1)S(1)} %copy-done.7), channel_id=1, source_target_pairs={{1,2},{2,1},{3,4},{4,3},{5,6},{6,5},{7,8},{8,7},{9,10},{10,9},{11,... | collective-permute-start | bytes 1572872 | tf_op jit(solution)/shard_map/ppermute | solution.py:269
  37.5 18.2 %all-to-all-start.1 = ((bf16[8,27,128]{2,1,0:T(8,128)(2,1)}), bf16[8,27,128]{2,1,0:T(8,128)(2,1)S(1)}, u32[]{:S(2)}, u32[]{:S(2)}) async-start(bf16[8,27,128]{2,1,0:T(8,128)(2,1)} %sum_rows.1), calls=%async_computation.1 | async-start | bytes 131072 | tf_op jit(solution)/shard_map/all_to_all | solution.py:320

commit v5 on v4

--- a/solution.py
+++ b/solution.py
@@ -72,12 +72,11 @@
     return [range(k, min(k + 2, 9 * kd + 9)) for k in range(9 * kd, 9 * kd + 9, 2)]
 
 
-def local_share_kernel(core, order, volume, cot, cot_near, cot_far, turned, share, wide, taps):
-    c = core[0]
-    cot_near[...] = cot[pl.ds(pl.multiple_of((1 - c) * CELLS, CELLS), CELLS), :]
-    cot_far[...] = cot[pl.ds(pl.multiple_of(c * CELLS, CELLS), CELLS), :]
+def local_share_kernel(order, volume, cot_in_hbm, turned, share, wide, taps, cot, sems):
+    (copy,) = start_all([(cot_in_hbm, cot)], sems)
     for i in range(SLAB):
         fill_taps(volume.at[i], i, wide, taps)
+    copy.wait()
     for j in range(SLAB * CELLS // 256):
         rows = pl.ds(j * 256, 256)
         turned[:, rows] = lax.dot_general(
@@ -94,9 +93,17 @@
 
 
 def local_share(*args):
-    plane = shaped(bf16, CELLS, COUT)
-    outs = (plane, plane, shaped(bf16, COUT, SLAB * CELLS), shaped(f32, COUT, COLUMNS))
-    return call(local_share_kernel, outs, args, taps_scratch(2), FLOPS * 2 // 3, name="local_share")
+    outs = (shaped(bf16, COUT, SLAB * CELLS), shaped(f32, COUT, COLUMNS))
+    own_copy = [pltpu.VMEM((SLAB * CELLS, COUT), bf16), pltpu.SemaphoreType.DMA((1,))]
+    return call(
+        local_share_kernel,
+        outs,
+        args,
+        taps_scratch(2) + own_copy,
+        FLOPS * 2 // 3,
+        specs=[IN_VMEM, IN_VMEM, IN_HBM],
+        name="local_share",
+    )
 
 
 def edge_share_kernel(core, near, far, turned, share, keep, send, wide, taps):
@@ -127,50 +134,47 @@
     return copies
 
 
-def forward_kernel(core, near, volume, far, weight_in_hbm, out, wide, taps, planes, weight, sems):
-    c = core[0]
-    step = pl.program_id(0)
-
-    @pl.when(step == 0)
-    def _():
-        own, *outer, whole = start_all(
-            [(volume, planes.at[pl.ds(0, SLAB)]), (near, planes.at[2]), (far, planes.at[3]), (weight_in_hbm, weight)],
-            sems,
-        )
-        own.wait()
-        for i in range(SLAB):
-            fill_taps(planes.at[i], 1 + i, wide, taps)
-        for copy in outer:
-            copy.wait()
-        fill_taps(planes.at[2], 3 * (1 - c), wide, taps)
-        fill_taps(planes.at[3], 3 * c, wide, taps)
-        whole.wait()
-
-    parts = []
-    for k in range(TAPS):
-        parts.append(taps[step + k // 9, pl.ds(k // 3 % 3 * SIDE, CELLS), pl.ds(k % 3 * CIN, CIN)])
-    pre = product(jnp.concatenate(parts, axis=1), weight[...])
-    out[...] = jnp.where(pre >= 0, pre, 0.3 * pre).astype(bf16)
-
-
-def forward(*args):
-    own_copies = [
+def forward_body(core, near, volume, far, weight_in_hbm, out, scratch, between):
+    planes, weight, result, sems = scratch[-4:]
+    wide, taps = scratch[:4], scratch[4:8]
+    first = core[0] == 0
+    *own, near_copy, far_copy, whole = start_all(
+        [
+            (volume.at[0], planes.at[0]),
+            (volume.at[1], planes.at[1]),
+            (near, planes.at[2]),
+            (far, planes.at[3]),
+            (weight_in_hbm, weight),
+        ],
+        sems,
+    )
+    for i in range(SLAB):
+        own[i].wait()
+        fill_taps(planes[i], 0, wide[1 + i], taps[1 + i])
+    near_copy.wait()
+    far_copy.wait()
+    fill_taps(jnp.where(first, planes[3], planes[2]), 0, wide[0], taps[0])
+    fill_taps(jnp.where(first, planes[2], planes[3]), 0, wide[3], taps[3])
+    whole.wait()
+    between()
+    writes = []
+    for d in range(SLAB):
+        parts = [taps[d + k // 9][0, pl.ds(k // 3 % 3 * SIDE, CELLS), pl.ds(k % 3 * CIN, CIN)] for k in range(TAPS)]
+        pre = product(jnp.concatenate(parts, axis=1), weight[...])
+        result[d] = jnp.where(pre >= 0, pre, 0.3 * pre).astype(bf16)
+        writes.append(pltpu.make_async_copy(result.at[d], out.at[pl.ds(d * CELLS, CELLS)], sems.at[5 + d]))
+        writes[d].start()
+    return writes
+
+
+def forward_scratch():
+    wide, taps = taps_scratch(1)
+    return [wide] * 4 + [taps] * 4 + [
         pltpu.VMEM((4, CELLS, CIN), bf16),
         pltpu.VMEM((COLUMNS, COUT), bf16),
-        pltpu.SemaphoreType.DMA((4,)),
+        pltpu.VMEM((SLAB, CELLS, COUT), bf16),
+        pltpu.SemaphoreType.DMA((7,)),
     ]
-    return call(
-        forward_kernel,
-        (shaped(bf16, SLAB * CELLS, COUT),),
-        args,
-        taps_scratch(4) + own_copies,
-        FLOPS,
-        specs=[IN_SMEM] + [IN_HBM] * 4,
-        grid=(SLAB,),
-        out_specs=(pl.BlockSpec((CELLS, COUT), lambda i: (i, 0)),),
-        vmem=VMEM_MOST,
-        name="forward",
-    )[0]
 
 
 def sum_rows_kernel(parts, rows, spread):
@@ -205,20 +209,21 @@
     return call(turn_weight_kernel, (shaped(bf16, 9 * COUT, 3 * CIN),), (weight,), name="turn_weight")[0]
 
 
-def input_grad_kernel(is_far, core, halo, cot, turned, *rest):
-    out, padded, weight, sums, result, sems = rest[-6:]
-    d = core[0] if is_far else 1 - core[0]
+def input_grad_copies(d, halo, cot, turned, scratch, whole):
+    padded, weight, _, _, sems = scratch
     middle = pl.ds(SIDE, CELLS)
-    planes = [
-        cot.at[pl.ds(pl.multiple_of(d * CELLS, CELLS), CELLS)],
-        cot.at[pl.ds(pl.multiple_of((1 - d) * CELLS, CELLS), CELLS)],
-        halo,
-    ]
+    mine = pl.ds(pl.multiple_of(d * CELLS, CELLS), CELLS)
+    other = pl.ds(pl.multiple_of((1 - d) * CELLS, CELLS), CELLS)
+    planes = [cot.at[mine], cot.at[other], halo.at[other] if whole else halo]
     pairs = []
     for slot, kd in enumerate((1, 2 * d, 2 - 2 * d)):
         rows = pl.ds(pl.multiple_of(kd * 3 * COUT, 3 * COUT), 3 * COUT)
         pairs += [(planes[slot], padded.at[slot, middle]), (turned.at[rows], weight.at[slot])]
-    copies = start_all(pairs, sems)
+    return start_all(pairs, sems)
+
+
+def input_grad_body(d, copies, out, scratch):
+    padded, weight, sums, result, sems = scratch
     zero = jnp.zeros((SIDE, COUT), bf16)
     inner = pl.ds(8, CELLS)
     for slot in range(3):
@@ -236,28 +241,64 @@
     result[...] = total.astype(bf16)
     write = pltpu.make_async_copy(result, out.at[pl.ds(pl.multiple_of(d * CELLS, CELLS), CELLS)], sems.at[6])
     write.start()
-    write.wait()
-
-
-def input_grad_plane(is_far, *args):
-    scratch = [
-        pltpu.VMEM((3, PADDED, COUT), bf16),
-        pltpu.VMEM((3, 3 * COUT, 3 * CIN), bf16),
-        pltpu.VMEM((CELLS + 16, 3 * CIN), f32),
-        pltpu.VMEM((CELLS, CIN), bf16),
-        pltpu.SemaphoreType.DMA((7,)),
-    ]
+    return write
+
+
+INPUT_GRAD_SCRATCH = [
+    pltpu.VMEM((3, PADDED, COUT), bf16),
+    pltpu.VMEM((3, 3 * COUT, 3 * CIN), bf16),
+    pltpu.VMEM((CELLS + 16, 3 * CIN), f32),
+    pltpu.VMEM((CELLS, CIN), bf16),
+    pltpu.SemaphoreType.DMA((7,)),
+]
+
+
+def near_kernel(core, near, volume, far, weight, halo, cot, turned, out, grad, *scratch):
+    d = 1 - core[0]
+    mine, other = scratch[:12], scratch[12:]
+    copies = []
+
+    def between():
+        copies.extend(input_grad_copies(d, halo, cot, turned, other, True))
+
+    writes = forward_body(core, near, volume, far, weight, out, mine, between)
+    writes.append(input_grad_body(d, copies, grad, other))
+    for write in writes:
+        write.wait()
+
+
+def forward_and_near(*args):
     return call(
-        functools.partial(input_grad_kernel, is_far),
+        near_kernel,
+        (shaped(bf16, SLAB * CELLS, COUT), shaped(bf16, SLAB * CELLS, CIN)),
+        args,
+        forward_scratch() + INPUT_GRAD_SCRATCH,
+        FLOPS * 3 // 2,
+        specs=[IN_SMEM] + [IN_HBM] * (len(args) - 1),
+        out_specs=(IN_HBM, IN_HBM),
+        vmem=VMEM_MORE,
+        name="forward_and_near",
+    )
+
+
+def far_kernel(core, halo, cot, turned, earlier, grad, *scratch):
+    d = core[0]
+    copies = input_grad_copies(d, halo, cot, turned, scratch, False)
+    input_grad_body(d, copies, grad, scratch).wait()
+
+
+def far_plane(*args):
+    return call(
+        far_kernel,
         (shaped(bf16, SLAB * CELLS, CIN),),
         args,
-        scratch,
+        INPUT_GRAD_SCRATCH,
         FLOPS // 2,
         specs=[IN_SMEM] + [IN_HBM] * (len(args) - 1),
         out_specs=(IN_HBM,),
-        input_output_aliases={4: 0} if len(args) > 4 else {},
+        input_output_aliases={4: 0},
         vmem=VMEM_MORE,
-        name="input_grad_far" if is_far else "input_grad_near",
+        name="input_grad_far",
     )[0]
 
 
@@ -295,15 +336,15 @@
 
     far, near, order = together(plane(core), plane(1 - core), row_order(flag))
     far, near = from_chip(far), from_core(near)
-    cot_near, cot_far, turned, share = local_share(flag, order, volume, cot)
+    turned, share = local_share(order, volume, cot)
     far, near, turned, share = together(far, near, turned, share)
     keep, send = edge_share(flag, near, far, turned, share)
 
     received = from_core(send)
     weight, send = together(weight, send)
     back_weight = turn_weight(weight)
-    cot_far, cot_near, back_weight = together(cot_far, cot_near, back_weight)
-    cot_far, cot_near = from_chip(cot_far), from_core(cot_near)
+    whole, back_weight = together(cot, back_weight)
+    cot_far, cot_near = from_chip(lax.dynamic_slice_in_dim(whole, core * CELLS, CELLS)), from_core(whole)
     received, back_weight = together(received, back_weight)
     total = keep + received.astype(f32)
 
@@ -311,15 +352,13 @@
     send = total.astype(bf16).reshape(dp, -1, COLUMNS)
     parts = lax.all_to_all(send, "dp", 0, 0)
     weight, send = together(weight, send)
-    activation = forward(flag, near, volume, far, weight)
-    back_weight, activation = together(back_weight, activation)
-    input_grad = input_grad_plane(False, flag, cot_near, cot, back_weight)
+    activation, input_grad = forward_and_near(flag, near, volume, far, weight, cot_near, cot, back_weight)
     parts, input_grad = together(parts, input_grad)
     send = sum_rows(parts)
 
     parts = lax.all_to_all(send, "space", 0, 0, axis_index_groups=[list(range(c, 16, 2)) for c in range(2)])
     back_weight, send = together(back_weight, send)
-    input_grad = input_grad_plane(True, flag, cot_far, cot, back_weight, input_grad)
+    input_grad = far_plane(flag, cot_far, cot, back_weight, input_grad)
     parts, input_grad = together(parts, input_grad)
     count = dp * lax.axis_size("space") * SLAB * CELLS
     return (

time: 57.2 us -> 57.2 us (level)
  the two profiles are of different devices: /device:TPU:6 before, /device:TPU:8 now
where the time goes in v5:
time: 57.2 us; the launch traced here: 56.7 us
  Pallas kernels  22.1 us (39%)
  starting transfers between devices  21.7 us (38%)
  waiting for transfers between devices  7.7 us (13%)
  local copies, waits for them, and re-layouts  3.33 us (6%)
  other arithmetic  1.05 us (2%)
  between operations  0.81 us (1%)
    pallas_call x8, Pallas kernels, call(): pl.pallas_call(kernel, out_shape=outs, in_specs=specs, scratch_shapes=lis...  22.1 us
    all_to_all x1, starting transfers between devices, shards(): lax.all_to_all(send, 'space', 0, 0, axis_index_groups=[list(range(c, 16,...  8.86 us
    all_to_all x1, starting transfers between devices, shards(): parts = lax.all_to_all(send, 'dp', 0, 0)  7.52 us
    ppermute x3, starting transfers between devices, from_core(): return lax.ppermute(value, 'space', [(i, i ^ 1) for i in range(16)])  3.94 us
    all_to_all x1, waiting for transfers between devices, shards(): parts = lax.all_to_all(send, 'dp', 0, 0)  3.87 us
    all_to_all x1, waiting for transfers between devices, shards(): lax.all_to_all(send, 'space', 0, 0, axis_index_groups=[list(range(c, 16,...  3.67 us
    unnamed x10, local copies, waits for them, and re-layouts  2.22 us
    ppermute x2, starting transfers between devices, from_chip(): lax.ppermute(value, 'space', [(i, (i + 1 ^ 1) - 1) for i in range(1, 15)])  1.37 us
  transfers between devices with their start and end apart: 7, of which 3 were waited for; matrix products, arithmetic and copies ran while one was open for 4% of the time, Pallas kernels for 34%

profile of v5, /device:TPU:8, one launch (start us, length us, event | category | flops | bytes accessed | tf_op | source)
XLA Modules:
  0.0 56.7 jit_solution(7990745377371695634)
XLA Ops:
  0.6 0.0 copy-start.2
  0.7 0.1 row_order.1.order
  0.7 1.0 %copy-done.2 = bf16[1,2,32,32,128]{4,3,2,1,0:T(8,128)(2,1)S(1)} copy-done((bf16[1,2,32,32,128]{4,3,2,1,0:T(8,128)(2,1)S(1)}, bf16[1,2,32,32,128]{4,3,2,1,0:T(8,128)(2,1)}, u32[]{:S(2)}) %copy-start.2) | copy-done | bytes 524312
  1.7 0.7 %collective-permute-start = (bf16[1024,128]{1,0:T(8,128)(2,1)S(1)}, bf16[1024,128]{1,0:T(8,128)(2,1)S(1)}, u32[]{:S(2)}, u32[]{:S(2)}) collective-permute-start(bf16[1024,128]{1,0:T(8,128)(2,1)S(1)} %get-tuple-element.27), channel_id=1, source_target_pairs={{1,2},{2,1},{3,4},{4,3},{5,6},{6,5},{7,8},{8,7},{9,10},{10,9},{11,... | collective-permute-start | bytes 786440 | tf_op jit(solution)/shard_map/ppermute | solution.py:310
  2.4 3.4 %collective-permute-start.1 = (bf16[1024,128]{1,0:T(8,128)(2,1)S(1)}, bf16[1024,128]{1,0:T(8,128)(2,1)S(1)}, u32[]{:S(2)}, u32[]{:S(2)}) collective-permute-start(bf16[1024,128]{1,0:T(8,128)(2,1)S(1)} %get-tuple-element.28), channel_id=1, source_target_pairs={{0,1},{1,0},{2,3},{3,2},{4,5},{5,4},{6,7},{7,6},{8,9},{9,8},{10,11... | collective-permute-start | bytes 786440 | tf_op jit(solution)/shard_map/ppermute | solution.py:306
  5.8 4.4 %local_share.1 = (bf16[256,2048]{1,0:T(8,128)(2,1)S(1)}, f32[256,3456]{1,0:T(8,128)S(1)}) custom-call(bf16[256,256]{1,0:T(8,128)(2,1)S(1)} %row_order.1.order, bf16[2,1024,128]{2,1,0:T(8,128)(2,1)S(1)} %bitcast.15, bf16[2048,256]{1,0:T(8,128)(2,1)} %bitcast.4.cot_in_hbm.cot), custom_call_target="tpu_custom_call" | custom-call | flops 2415919104 | bytes 4194304 | tf_op jit(solution)/shard_map/local_share/pallas_call | solution.py:33
  10.2 0.0 collective-permute-done.far
  10.2 0.0 collective-permute-done.1.near
  10.2 0.0 copy-start.3
  10.2 0.0 copy-start
  10.2 1.9 %edge_share.1 = (f32[128,3456]{1,0:T(8,128)S(1)}, bf16[128,3456]{1,0:T(8,128)(2,1)S(1)}) custom-call(s32[1]{0:T(128)} %bitcast.core, bf16[1024,128]{1,0:T(8,128)(2,1)S(1)} %collective-permute-done.1.near, bf16[1024,128]{1,0:T(8,128)(2,1)S(1)} %collective-permute-done.far, bf16[256,2048]{1,0:T(8,128)(2,1)S(1)} %get-tuple-element.34.turned, ...), custom_call_target="tpu_custom_call" | custom-call | flops 1207959552 | bytes 4194304 | tf_op jit(solution)/shard_map/edge_share/pallas_call | solution.py:33
  12.2 0.0 copy-done.3
  12.2 0.1 collective-permute-start.2
  12.3 0.0 copy-done
  12.3 0.5 turn_weight.1.turned
  12.8 0.0 copy-start.1
  12.8 1.2 %copy-done.1 = bf16[2304,384]{1,0:T(8,128)(2,1)} copy-done((bf16[2304,384]{1,0:T(8,128)(2,1)}, bf16[2304,384]{1,0:T(8,128)(2,1)S(1)}, u32[]{:S(2)}) %copy-start.1) | copy-done | bytes 1769496
  14.1 0.5 collective-permute-start.3
  14.5 0.2 collective-permute-done.2
  14.7 1.1 %fusion = bf16[16,8,3456]{2,1,0:T(8,128)(2,1)} fusion(f32[128,3456]{1,0:T(8,128)S(1)} %get-tuple-element.38, bf16[128,3456]{1,0:T(8,128)(2,1)S(1)} %collective-permute-done.2), kind=kLoop, calls=%fused_computation.1 | loop fusion | flops 1327104 | bytes 3538944 | tf_op jit(solution)/shard_map/reshape | solution.py:352
  15.8 7.5 %all-to-all-start = ((bf16[16,8,3456]{2,1,0:T(8,128)(2,1)}), bf16[16,8,3456]{2,1,0:T(8,128)(2,1)S(1)}, u32[]{:S(2)}, u32[]{:S(2)}) async-start(bf16[16,8,3456]{2,1,0:T(8,128)(2,1)} %fusion), calls=%async_computation | async-start | bytes 1769472 | tf_op jit(solution)/shard_map/all_to_all | solution.py:353
  23.3 1.1 %constant_dynamic-slice_fusion = bf16[1024,256]{1,0:T(8,128)(2,1)S(1)} fusion(bf16[2048,256]{1,0:T(8,128)(2,1)} %bitcast.4.cot_in_hbm.cot, s32[]{:T(128)S(6)} %select_n.20), kind=kLoop, calls=%fused_computation.4 | loop fusion | bytes 1048580 | tf_op jit(solution)/shard_map/dynamic_slice | solution.py:347
  24.4 0.7 %collective-permute-start.4 = (bf16[1024,256]{1,0:T(8,128)(2,1)S(1)}, bf16[1024,256]{1,0:T(8,128)(2,1)S(1)}, u32[]{:S(2)}, u32[]{:S(2)}) collective-permute-start(bf16[1024,256]{1,0:T(8,128)(2,1)S(1)} %constant_dynamic-slice_fusion), channel_id=1, source_target_pairs={{1,2},{2,1},{3,4},{4,3},{5,6},{6,5},{7,8},{8,7},{9,10},{10,9},{11,... | collective-permute-start | bytes 1572872 | tf_op jit(solution)/shard_map/ppermute | solution.py:310
  25.1 0.0 collective-permute-done.3.halo
  25.1 9.1 %forward_and_near.1 = (bf16[2048,256]{1,0:T(8,128)(2,1)}, bf16[2048,128]{1,0:T(8,128)(2,1)}) custom-call(s32[1]{0:T(128)} %bitcast.core, bf16[1024,128]{1,0:T(8,128)(2,1)S(1)} %copy-done.4, bf16[2,1024,128]{2,1,0:T(8,128)(2,1)S(1)} %bitcast.16, bf16[1024,128]{1,0:T(8,128)(2,1)S(1)} %collective-permute-done.far, bf16[3456,256]{1,0:T(8,128)(2,1)} %bitcast.12, ...), custom_call_target="tpu_custom_call" | custom-call | flops 5435817984 | bytes 4194304 | tf_op jit(solution)/shard_map/forward_and_near/pallas_call | solution.py:33
  34.2 3.9 %all-to-all-done.parts = bf16[16,8,3456]{2,1,0:T(8,128)(2,1)S(1)} async-done(((bf16[16,8,3456]{2,1,0:T(8,128)(2,1)}), bf16[16,8,3456]{2,1,0:T(8,128)(2,1)S(1)}, u32[]{:S(2)}, u32[]{:S(2)}) %all-to-all-start) | async-done | bytes 884768 | tf_op jit(solution)/shard_map/all_to_all | solution.py:353
  38.0 0.8 %sum_rows.1 = bf16[8,27,128]{2,1,0:T(8,128)(2,1)} custom-call(bf16[16,8,3456]{2,1,0:T(8,128)(2,1)S(1)} %all-to-all-done.parts), custom_call_target="tpu_custom_call" | custom-call | flops 1048576 | bytes 4194304 | tf_op jit(solution)/shard_map/sum_rows/pallas_call | solution.py:33
  38.8 8.9 %all-to-all-start.1 = ((bf16[8,27,128]{2,1,0:T(8,128)(2,1)}), bf16[8,27,128]{2,1,0:T(8,128)(2,1)S(1)}, u32[]{:S(2)}, u32[]{:S(2)}) async-start(bf16[8,27,128]{2,1,0:T(8,128)(2,1)} %sum_rows.1), calls=%async_computation.1 | async-start | bytes 131072 | tf_op jit(solution)/shard_map/all_to_all | solution.py:359
  47.7 0.0 collective-permute-done.4.halo
  47.7 4.7 %input_grad_far.1 = bf16[2048,128]{1,0:T(8,128)(2,1)} custom-call(s32[1]{0:T(128)} %bitcast.core, bf16[1024,256]{1,0:T(8,128)(2,1)S(1)} %collective-permute-done.4.halo, bf16[2048,256]{1,0:T(8,128)(2,1)} %bitcast.4.cot_in_hbm.cot, bf16[2304,384]{1,0:T(8,128)(2,1)} %copy-done.1, ...), custom_call_target="tpu_custom_call", output_to_operand_aliasing={{}: (4, {})} | custom-call | flops 1811939328 | bytes 4194304 | tf_op jit(solution)/shard_map/input_grad_far/pallas_call | solution.py:33
  52.4 3.7 %all-to-all-done.1.parts = bf16[8,27,128]{2,1,0:T(8,128)(2,1)S(1)} async-done(((bf16[8,27,128]{2,1,0:T(8,128)(2,1)}), bf16[8,27,128]{2,1,0:T(8,128)(2,1)S(1)}, u32[]{:S(2)}, u32[]{:S(2)}) %all-to-all-start.1) | async-done | bytes 55328 | tf_op jit(solution)/shard_map/all_to_all | solution.py:359
  56.1 0.6 %finish.1 = f32[1,3456]{1,0:T(1,128)} custom-call(bf16[8,27,128]{2,1,0:T(8,128)(2,1)S(1)} %all-to-all-done.1.parts), custom_call_target="tpu_custom_call" | custom-call | flops 1048576 | bytes 4194304 | tf_op jit(solution)/shard_map/finish/pallas_call | solution.py:33
  (3 shorter events, 0.0 us)
Async XLA Ops:
  0.6 1.0 %copy-start.2 = (bf16[1,2,32,32,128]{4,3,2,1,0:T(8,128)(2,1)S(1)}, bf16[1,2,32,32,128]{4,3,2,1,0:T(8,128)(2,1)}, u32[]{:S(2)}) copy-start(bf16[1,2,32,32,128]{4,3,2,1,0:T(8,128)(2,1)} %param.3) | copy-start | bytes 1572868
  1.7 8.5 %collective-permute-start = (bf16[1024,128]{1,0:T(8,128)(2,1)S(1)}, bf16[1024,128]{1,0:T(8,128)(2,1)S(1)}, u32[]{:S(2)}, u32[]{:S(2)}) collective-permute-start(bf16[1024,128]{1,0:T(8,128)(2,1)S(1)} %get-tuple-element.27), channel_id=1, source_target_pairs={{1,2},{2,1},{3,4},{4,3},{5,6},{6,5},{7,8},{8,7},{9,10},{10,9},{11,... | collective-permute-start | bytes 786440 | tf_op jit(solution)/shard_map/ppermute | solution.py:310
  2.4 7.8 %collective-permute-start.1 = (bf16[1024,128]{1,0:T(8,128)(2,1)S(1)}, bf16[1024,128]{1,0:T(8,128)(2,1)S(1)}, u32[]{:S(2)}, u32[]{:S(2)}) collective-permute-start(bf16[1024,128]{1,0:T(8,128)(2,1)S(1)} %get-tuple-element.28), channel_id=1, source_target_pairs={{0,1},{1,0},{2,3},{3,2},{4,5},{5,4},{6,7},{7,6},{8,9},{9,8},{10,11... | collective-permute-start | bytes 786440 | tf_op jit(solution)/shard_map/ppermute | solution.py:306
  10.2 2.0 %copy-start.3 = (bf16[1024,128]{1,0:T(8,128)(2,1)}, bf16[1024,128]{1,0:T(8,128)(2,1)S(1)}, u32[]{:S(2)}) copy-start(bf16[1024,128]{1,0:T(8,128)(2,1)S(1)} %collective-permute-done.1.near) | copy-start | bytes 786436
  10.2 2.1 %copy-start = (bf16[27,128,256]{2,1,0:T(8,128)(2,1)S(1)}, bf16[27,128,256]{2,1,0:T(8,128)(2,1)}, u32[]{:S(2)}) copy-start(bf16[27,128,256]{2,1,0:T(8,128)(2,1)} %param.4) | copy-start | bytes 5308420
  12.2 2.5 %collective-permute-start.2 = (bf16[128,3456]{1,0:T(8,128)(2,1)S(1)}, bf16[128,3456]{1,0:T(8,128)(2,1)S(1)}, u32[]{:S(2)}, u32[]{:S(2)}) collective-permute-start(bf16[128,3456]{1,0:T(8,128)(2,1)S(1)} %get-tuple-element.36), channel_id=1, source_target_pairs={{0,1},{1,0},{2,3},{3,2},{4,5},{5,4},{6,7},{7,6},{8,9},{9,8},{10,11... | collective-permute-start | bytes 2654216 | tf_op jit(solution)/shard_map/ppermute | solution.py:306
  12.8 1.2 %copy-start.1 = (bf16[2304,384]{1,0:T(8,128)(2,1)}, bf16[2304,384]{1,0:T(8,128)(2,1)S(1)}, u32[]{:S(2)}) copy-start(bf16[2304,384]{1,0:T(8,128)(2,1)S(1)} %turn_weight.1.turned) | copy-start | bytes 5308420
  14.1 11.0 %collective-permute-start.3 = (bf16[2048,256]{1,0:T(8,128)(2,1)}, bf16[2048,256]{1,0:T(8,128)(2,1)}, u32[]{:S(2)}, u32[]{:S(2)}) collective-permute-start(bf16[2048,256]{1,0:T(8,128)(2,1)} %bitcast.4.cot_in_hbm.cot), channel_id=1, source_target_pairs={{0,1},{1,0},{2,3},{3,2},{4,5},{5,4},{6,7},{7,6},{8,9},{9,8},{10,11... | collective-permute-start | bytes 3145736 | tf_op jit(solution)/shard_map/ppermute | solution.py:306
  15.8 9.3 %copy-start.4 = (bf16[1024,128]{1,0:T(8,128)(2,1)S(1)}, bf16[1024,128]{1,0:T(8,128)(2,1)}, u32[]{:S(2)}) copy-start(bf16[1024,128]{1,0:T(8,128)(2,1)} %copy-done.3) | copy-start | bytes 786436
  15.8 22.3 %all-to-all-start = ((bf16[16,8,3456]{2,1,0:T(8,128)(2,1)}), bf16[16,8,3456]{2,1,0:T(8,128)(2,1)S(1)}, u32[]{:S(2)}, u32[]{:S(2)}) async-start(bf16[16,8,3456]{2,1,0:T(8,128)(2,1)} %fusion), calls=%async_computation | async-start | bytes 1769472 | tf_op jit(solution)/shard_map/all_to_all | solution.py:353
  24.4 23.3 %collective-permute-start.4 = (bf16[1024,256]{1,0:T(8,128)(2,1)S(1)}, bf16[1024,256]{1,0:T(8,128)(2,1)S(1)}, u32[]{:S(2)}, u32[]{:S(2)}) collective-permute-start(bf16[1024,256]{1,0:T(8,128)(2,1)S(1)} %constant_dynamic-slice_fusion), channel_id=1, source_target_pairs={{1,2},{2,1},{3,4},{4,3},{5,6},{6,5},{7,8},{8,7},{9,10},{10,9},{11,... | collective-permute-start | bytes 1572872 | tf_op jit(solution)/shard_map/ppermute | solution.py:310
  38.8 17.2 %all-to-all-start.1 = ((bf16[8,27,128]{2,1,0:T(8,128)(2,1)}), bf16[8,27,128]{2,1,0:T(8,128)(2,1)S(1)}, u32[]{:S(2)}, u32[]{:S(2)}) async-start(bf16[8,27,128]{2,1,0:T(8,128)(2,1)} %sum_rows.1), calls=%async_computation.1 | async-start | bytes 131072 | tf_op jit(solution)/shard_map/all_to_all | solution.py:359
